TPU v7x, 128 devices: a whole 4x4x4 slice. The times are simulated.
128 devices in a mesh: dp: 8 (over y_lo, z), expert: 16 (over x, y_hi, core).
Axes of the slice: x: 4, y: 4 (y_hi: 2, y_lo: 2; y = y_hi * 2 + y_lo), z: 4, core: 2. Of those that a mesh axis runs over, the one named last changes fastest.
Arguments:
- tokens: bfloat16 [16384, 4096], P(('dp', 'expert')), may hold values from -6 to 6
- up_grad: bfloat16 [16384, 8, 1536], P(('dp', 'expert')), may hold values from -6 to 6
- gate_weights: float32 [16384, 8], P(('dp', 'expert')), may hold values from 0.02 to 0.3
- expert_ids: int32 [16384, 8], P(('dp', 'expert')), may hold values from 0 to 127, all different within a row; in each aligned block of 128 rows (0 to 127, 128 to 255, ...) at most 10 rows name the same one
- new_home: int32 [128], replicated, may hold values from 0 to 127, as said below
- adapter_a: float32 [128, 32, 4096], P('expert'), may hold values from -0.09375 to 0.09375
- adapter_b: float32 [128, 32, 1536], P('expert'), may hold values from -0.15625 to 0.15625
- first_moment: float32 [128, 180224], P('expert', 'dp'), may hold values from -4 to 4
- second_moment: float32 [128, 180224], P('expert', 'dp'), may hold values from 0.01 to 1
Outputs:
- new_a: float32 [128, 32, 4096], P('expert')
- new_b: float32 [128, 32, 1536], P('expert')
- new_first: float32 [128, 180224], P('expert', 'dp')
- new_second: float32 [128, 180224], P('expert', 'dp')
Inputs may be any that keep to these rules, and one draw needn't show every extreme that they name: `expert_ids`: each row names 8 different experts. Among the 128 rows of one device no expert is named by more than 10 rows, a bound that some block reaches. `new_home`: a permutation. Slot s lies on device s // 8 of the expert axis; expert e starts in slot e and ends in slot new_home[e]. Between two different devices at most one expert moves, and some pair has exactly one; every device sends as many experts to other devices as it receives, and all devices the same number.
All inputs are finite; a program needn't handle non-finite values.
Results may differ from a plain program's by a relative error of at most 0.0048.
Values may be sent and summed in bfloat16 or wider, within the bound.
A program may use at most 192 MiB of HBM per device.

v0:
```python
import jax
import jax.numpy as jnp
from jax import lax
from jax.sharding import PartitionSpec as P

beta_one = 0.9
beta_two = 0.999
learn_rate = 0.001
decay_rate = 0.01
adam_eps = 1e-08
adapter_scale_factor = 2.0
adam_step = 10.0


def route_rows(tokens, up_grad, gate_weights, expert_ids, homes, capacity, local, devices):
    top = expert_ids.shape[1]
    slots = expert_ids.shape[0] * top
    experts = homes.shape[0]
    width = tokens.shape[1]
    hidden = up_grad.shape[2]
    flat_ids = expert_ids.reshape(slots)
    hits = (flat_ids[:, None] == jnp.arange(experts, dtype=jnp.int32)[None, :]).astype(jnp.int32)
    target = jnp.sum(hits * homes[None, :], axis=1)
    earlier = jnp.cumsum(hits, axis=0) - hits
    position = jnp.sum(earlier * hits, axis=1)
    row_index = target * capacity + position
    cotangent = (
        (gate_weights[:, :, None] * up_grad.astype(jnp.float32))
        .astype(jnp.bfloat16)
        .reshape(slots, hidden)
    )
    copies = jnp.repeat(tokens, top, axis=0)
    send_rows = jnp.zeros((experts * capacity, width), jnp.bfloat16).at[row_index].set(copies)
    send_cots = jnp.zeros((experts * capacity, hidden), jnp.bfloat16).at[row_index].set(cotangent)
    got_rows, got_cots = (
        lax.all_to_all(send_rows, "expert", split_axis=0, concat_axis=0, tiled=True),
        lax.all_to_all(send_cots, "expert", split_axis=0, concat_axis=0, tiled=True),
    )
    return (
        got_rows.reshape(devices, local, capacity, width),
        got_cots.reshape(devices, local, capacity, hidden),
    )


def group_gradients(got_rows, got_cots, a_now, b_now):
    local = a_now.shape[0]
    a16 = a_now.astype(jnp.bfloat16)
    b16 = b_now.astype(jnp.bfloat16)
    low_rank_hidden = jnp.einsum(
        "pjcd,jrd->pjcr", got_rows, a16, preferred_element_type=jnp.float32
    ).astype(jnp.bfloat16)
    backward_rows = jnp.einsum(
        "pjcf,jrf->pjcr", got_cots, b16, preferred_element_type=jnp.float32
    ).astype(jnp.bfloat16)
    down_adapter_gradient = jnp.einsum(
        "pjcr,pjcd->jrd", backward_rows, got_rows, preferred_element_type=jnp.float32
    )
    up_adapter_gradient = jnp.einsum(
        "pjcr,pjcf->jrf", low_rank_hidden, got_cots, preferred_element_type=jnp.float32
    )
    flat = jnp.concatenate(
        [down_adapter_gradient.reshape(local, -1), up_adapter_gradient.reshape(local, -1)], axis=1
    )
    gradient_total = lax.psum_scatter(flat, "dp", scatter_dimension=1, tiled=True)
    return adapter_scale_factor * gradient_total


def own_share(a_now, b_now):
    local = a_now.shape[0]
    flat = jnp.concatenate([a_now.reshape(local, -1), b_now.reshape(local, -1)], axis=1)
    share = flat.shape[1] // lax.axis_size("dp")
    return lax.dynamic_slice_in_dim(flat, lax.axis_index("dp") * share, share, 1)


def adamw_step(grad_share, param_share, first, second):
    fix_one = 1.0 - beta_one**adam_step
    fix_two = 1.0 - beta_two**adam_step
    first_out = beta_one * first + (1.0 - beta_one) * grad_share
    second_out = beta_two * second + (1.0 - beta_two) * grad_share * grad_share
    param_out = param_share - learn_rate * (
        first_out / fix_one / (jnp.sqrt(second_out / fix_two) + adam_eps) + decay_rate * param_share
    )
    return (param_out, first_out, second_out)


def regather(param_share, rank, width, hidden):
    local = param_share.shape[0]
    whole = lax.all_gather(param_share, "dp", axis=1, tiled=True)
    return (
        whole[:, : rank * width].reshape(local, rank, width),
        whole[:, rank * width :].reshape(local, rank, hidden),
    )


def outgoing(array, source_place, has_one):
    picked = array[source_place]
    mask = has_one.reshape((has_one.shape[0],) + (1,) * (array.ndim - 1))
    return jnp.where(mask, picked, jnp.zeros((), array.dtype))


def incoming(local_array, received, pick_index):
    return jnp.concatenate([local_array, received], axis=0)[pick_index]


def shards(
    tokens,
    up_grad,
    gate_weights,
    expert_ids,
    new_home,
    adapter_a,
    adapter_b,
    first_moment,
    second_moment,
):
    local = adapter_a.shape[0]
    rank = adapter_a.shape[1]
    width = adapter_a.shape[2]
    hidden = adapter_b.shape[2]
    experts = new_home.shape[0]
    devices = lax.axis_size("expert")
    myself = lax.axis_index("expert")
    capacity = expert_ids.shape[0] * expert_ids.shape[1] * 5 // (4 * experts)
    places = jnp.arange(local, dtype=jnp.int32)
    peers = jnp.arange(devices, dtype=jnp.int32)
    owner = jnp.zeros((experts,), jnp.int32).at[new_home].set(jnp.arange(experts, dtype=jnp.int32))
    target_device = lax.dynamic_slice_in_dim(new_home, myself * local, local, 0) // local
    leaving = (target_device[None, :] == peers[:, None]) & (target_device[None, :] != myself)
    source_place = jnp.sum(leaving.astype(jnp.int32) * places[None, :], axis=1)
    has_one = jnp.any(leaving, axis=1)
    arriving = lax.dynamic_slice_in_dim(owner, myself * local, local, 0)
    from_device = arriving // local
    pick_index = jnp.where(from_device == myself, arriving % local, local + from_device)
    sent = (
        lax.all_to_all(
            outgoing(adapter_a, source_place, has_one),
            "expert",
            split_axis=0,
            concat_axis=0,
            tiled=True,
        ),
        lax.all_to_all(
            outgoing(adapter_b, source_place, has_one),
            "expert",
            split_axis=0,
            concat_axis=0,
            tiled=True,
        ),
        lax.all_to_all(
            outgoing(first_moment, source_place, has_one),
            "expert",
            split_axis=0,
            concat_axis=0,
            tiled=True,
        ),
        lax.all_to_all(
            outgoing(second_moment, source_place, has_one),
            "expert",
            split_axis=0,
            concat_axis=0,
            tiled=True,
        ),
    )
    a_now = incoming(adapter_a, sent[0], pick_index)
    b_now = incoming(adapter_b, sent[1], pick_index)
    first_now = incoming(first_moment, sent[2], pick_index)
    second_now = incoming(second_moment, sent[3], pick_index)
    got_rows, got_cots = route_rows(
        tokens, up_grad, gate_weights, expert_ids, new_home, capacity, local, devices
    )
    grad_share = group_gradients(got_rows, got_cots, a_now, b_now)
    param_out, first_out, second_out = adamw_step(
        grad_share, own_share(a_now, b_now), first_now, second_now
    )
    new_a, new_b = regather(param_out, rank, width, hidden)
    return (new_a, new_b, first_out, second_out)


def solution(mesh):
    placed = (
        P(("dp", "expert"), None),
        P(("dp", "expert"), None, None),
        P(("dp", "expert"), None),
        P(("dp", "expert"), None),
        P(),
        P("expert", None, None),
        P("expert", None, None),
        P("expert", "dp"),
        P("expert", "dp"),
    )
    return jax.shard_map(
        shards,
        mesh=mesh,
        in_specs=placed,
        out_specs=(
            P("expert", None, None),
            P("expert", None, None),
            P("expert", "dp"),
            P("expert", "dp"),
        ),
        check_vma=False,
    )
```

profile of v0, /device:TPU:1, one launch (start us, length us, event | category | flops | bytes accessed | tf_op | source)
XLA Modules:
  0.0 676.6 jit_solution(15975154598481069800)
XLA Ops:
  16.0 8.6 %all-to-all-start.1 = ((f32[16,32,1536]{2,1,0:T(8,128)}), f32[16,32,1536]{2,1,0:T(8,128)}, u32[]{:S(2)}, u32[]{:S(2)}) async-start(f32[16,32,1536]{2,1,0:T(8,128)} %broadcast_select_fusion.1), calls=%async_computation.1 | async-start | bytes 6291456 | tf_op jit(solution)/shard_map/all_to_all | solution.py:142
  26.0 8.8 %scatter_custom_fusion.1 = bf16[1280,1536]{1,0:T(8,128)(2,1)} fusion(s32[1024]{0:T(1024)S(1)} %bitcast.98, bf16[128,8,1536]{2,1,0:T(8,128)(2,1)} %param.10, f32[128,8]{1,0:T(8,128)S(1)} %copy.41, bf16[]{:T(256)} %constant.88.clone.1), kind=kCustom, calls=%fused_computation.24 | custom fusion | flops 4718592 | bytes 7143426 | tf_op jit(solution)/shard_map/scatter | solution.py:34
  34.9 29.6 %all-to-all-done.1 = f32[16,32,1536]{2,1,0:T(8,128)} async-done(((f32[16,32,1536]{2,1,0:T(8,128)}), f32[16,32,1536]{2,1,0:T(8,128)}, u32[]{:S(2)}, u32[]{:S(2)}) %all-to-all-start.1) | async-done | bytes 3145760 | tf_op jit(solution)/shard_map/all_to_all | solution.py:142
  64.4 9.4 %all-to-all-start.3 = ((bf16[16,80,1536]{2,1,0:T(8,128)(2,1)}), bf16[16,80,1536]{2,1,0:T(8,128)(2,1)}, u32[]{:S(2)}, u32[]{:S(2)}) async-start(bf16[16,80,1536]{2,1,0:T(8,128)(2,1)} %bitcast.91), calls=%async_computation.3 | async-start | bytes 7864320 | tf_op jit(solution)/shard_map/all_to_all | solution.py:37
  73.9 6.5 gather_fusion
  80.4 8.0 %broadcast_select_fusion = f32[16,32,4096]{2,1,0:T(8,128)} fusion(f32[16,32,4096]{2,1,0:T(8,128)} %gather_fusion, pred[16]{0:T(512)(128)(4,1)S(1)} %fusion.32), kind=kLoop, calls=%fused_computation.22 | loop fusion | flops 2097152 | bytes 16777232 | tf_op jit(solution)/shard_map/jit(_where)/select_n | solution.py:98
  88.3 34.9 %all-to-all-done.3 = bf16[16,80,1536]{2,1,0:T(8,128)(2,1)} async-done(((bf16[16,80,1536]{2,1,0:T(8,128)(2,1)}), bf16[16,80,1536]{2,1,0:T(8,128)(2,1)}, u32[]{:S(2)}, u32[]{:S(2)}) %all-to-all-start.3) | async-done | bytes 3932192 | tf_op jit(solution)/shard_map/all_to_all | solution.py:37
  123.3 12.5 %all-to-all-start = ((f32[16,32,4096]{2,1,0:T(8,128)}), f32[16,32,4096]{2,1,0:T(8,128)}, u32[]{:S(2)}, u32[]{:S(2)}) async-start(f32[16,32,4096]{2,1,0:T(8,128)} %broadcast_select_fusion), calls=%async_computation | async-start | bytes 16777216 | tf_op jit(solution)/shard_map/all_to_all | solution.py:135
  135.7 17.1 %scatter_custom_fusion.2 = bf16[1280,4096]{1,0:T(8,128)(2,1)} fusion(s32[1024]{0:T(1024)S(1)} %bitcast.99, bf16[]{:T(256)} %constant.88.clone.1, bf16[128,4096]{1,0:T(8,128)(2,1)S(1)} %copy-done), kind=kCustom, calls=%fused_computation.12 | custom fusion | bytes 11534338 | tf_op jit(solution)/shard_map/scatter | solution.py:33
  152.8 113.9 %all-to-all-done = f32[16,32,4096]{2,1,0:T(8,128)} async-done(((f32[16,32,4096]{2,1,0:T(8,128)}), f32[16,32,4096]{2,1,0:T(8,128)}, u32[]{:S(2)}, u32[]{:S(2)}) %all-to-all-start) | async-done | bytes 8388640 | tf_op jit(solution)/shard_map/all_to_all | solution.py:135
  266.7 9.6 %all-to-all-start.4 = ((bf16[16,80,4096]{2,1,0:T(8,128)(2,1)}), bf16[16,80,4096]{2,1,0:T(8,128)(2,1)}, u32[]{:S(2)}, u32[]{:S(2)}) async-start(bf16[16,80,4096]{2,1,0:T(8,128)(2,1)} %bitcast.83), calls=%async_computation.4 | async-start | bytes 20971520 | tf_op jit(solution)/shard_map/all_to_all | solution.py:36
  285.3 6.1 copy.42
  291.4 10.7 %pad_maximum_fusion = f32[24,32,4096]{2,1,0:T(8,128)} fusion(f32[16,32,4096]{2,1,0:T(8,128)} %all-to-all-done, f32[8,32,4096]{2,1,0:T(8,128)} %param.14), kind=kLoop, calls=%fused_computation.11 | loop fusion | flops 3145728 | bytes 25165824 | tf_op jit(solution)/shard_map/concatenate | solution.py:102
  302.1 7.4 %gather_fusion.1 = f32[8,32,4096]{2,1,0:T(8,128)} fusion(f32[24,32,4096]{2,1,0:T(8,128)} %pad_maximum_fusion, s32[1024]{0:T(1024)S(1)} %pad_clamp_fusion), kind=kCustom, calls=%fused_computation.1 | custom fusion | bytes 8388640 | tf_op jit(solution)/shard_map/gather | solution.py:102
  309.5 132.7 %all-to-all-done.4 = bf16[16,80,4096]{2,1,0:T(8,128)(2,1)} async-done(((bf16[16,80,4096]{2,1,0:T(8,128)(2,1)}), bf16[16,80,4096]{2,1,0:T(8,128)(2,1)}, u32[]{:S(2)}, u32[]{:S(2)}) %all-to-all-start.4) | async-done | bytes 10485792 | tf_op jit(solution)/shard_map/all_to_all | solution.py:36
  442.1 13.7 %copy.43 = bf16[16,80,4096]{2,0,1:T(8,128)(2,1)} copy(bf16[16,80,4096]{2,1,0:T(8,128)(2,1)} %all-to-all-done.4) | data formatting | bytes 20971520 | tf_op jit(solution)/shard_map/all_to_all | solution.py:36
  455.8 11.2 %convolution_bitcast_fusion.1 = f32[1,8,32,1536]{3,2,1,0:T(8,128)} fusion(bf16[16,8,10,1536]{3,0,2,1:T(8,128)(2,1)} %bitcast.85, bf16[16,8,10,4096]{3,0,2,1:T(8,128)(2,1)} %bitcast.81, f32[8,32,4096]{2,1,0:T(8,128)} %gather_fusion.1), kind=kOutput, calls=%fused_computation.26 | convolution fusion | flops 462462976 | bytes 20185088 | tf_op jit(solution)/shard_map/pjcr,pjcf->jrf/dot_general | solution.py:58
  470.5 9.8 %convolution_bitcast_fusion = f32[1,8,32,4096]{3,2,1,0:T(8,128)} fusion(bf16[16,8,10,4096]{3,0,2,1:T(8,128)(2,1)} %bitcast.82, bf16[16,8,10,1536]{3,0,2,1:T(8,128)(2,1)} %bitcast.86, f32[8,32,1536]{2,1,0:T(8,128)S(1)} %gather_fusion.3), kind=kOutput, calls=%fused_computation.18 | convolution fusion | flops 461807616 | bytes 20185088 | tf_op jit(solution)/shard_map/pjcr,pjcd->jrd/dot_general | solution.py:55
  500.4 8.5 %all-to-all-start.2 = ((f32[16,1,22528]{2,1,0:T(1,128)}), f32[16,1,22528]{2,1,0:T(1,128)}, u32[]{:S(2)}, u32[]{:S(2)}) async-start(f32[16,1,22528]{2,1,0:T(1,128)} %copy.36), calls=%async_computation.2 | async-start | bytes 2883584 | tf_op jit(solution)/shard_map/all_to_all | solution.py:149
  512.9 20.0 %all-to-all-done.2 = f32[16,1,22528]{2,1,0:T(1,128)} async-done(((f32[16,1,22528]{2,1,0:T(1,128)}), f32[16,1,22528]{2,1,0:T(1,128)}, u32[]{:S(2)}, u32[]{:S(2)}) %all-to-all-start.2) | async-done | bytes 1441824 | tf_op jit(solution)/shard_map/all_to_all | solution.py:149
  543.7 18.1 %all-to-all-done.5 = f32[16,1,22528]{2,1,0:T(1,128)} async-done(((f32[16,1,22528]{2,1,0:T(1,128)}), f32[16,1,22528]{2,1,0:T(1,128)}, u32[]{:S(2)}, u32[]{:S(2)}) %all-to-all-start.5) | async-done | bytes 1441824 | tf_op jit(solution)/shard_map/all_to_all | solution.py:156
  570.6 6.8 %copy.53 = f32[1,8,32,4096]{3,1,2,0:T(8,128)} copy(f32[1,8,32,4096]{3,2,1,0:T(8,128)} %bitcast.84) | data formatting | bytes 8388608
  577.4 14.2 %reduce-scatter.2.cloned.1.call-done = f32[8,22528]{1,0:T(8,128)} async-done(((f32[8,180224]{1,0:T(8,128)}), f32[8,22528]{1,0:T(8,128)}) %reduce-scatter.2.cloned.1.call-update) | async-done | bytes 720912 | tf_op jit(solution)/shard_map/reduce_scatter | solution.py:64
  594.8 66.1 %all-gather.2.cloned.1.call-done = f32[8,180224]{1,0:T(8,128)} async-done(((f32[8,22528]{1,0:T(8,128)}), f32[8,180224]{1,0:T(8,128)}) %all-gather.2.cloned.1.call-update) | async-done | bytes 5767184 | tf_op jit(solution)/shard_map/all_gather | solution.py:88
  (77 shorter events, 78.1 us)
Async XLA Ops:
  7.2 128.6 %copy-start = (bf16[128,4096]{1,0:T(8,128)(2,1)S(1)}, bf16[128,4096]{1,0:T(8,128)(2,1)}, u32[]{:S(2)}) copy-start(bf16[128,4096]{1,0:T(8,128)(2,1)} %param.9) | copy-start | bytes 3145732
  16.0 8.6 %copy-start.8 = (s32[128,8]{0,1:T(8,128)S(1)}, s32[128,8]{0,1:T(8,128)}, u32[]{:S(2)}) copy-start(s32[128,8]{0,1:T(8,128)} %param.12) | copy-start | bytes 12292
  16.0 9.4 %copy-start.9 = (f32[128,8]{0,1:T(8,128)S(1)}, f32[128,8]{0,1:T(8,128)}, u32[]{:S(2)}) copy-start(f32[128,8]{0,1:T(8,128)} %param.11) | copy-start | bytes 12292
  16.0 9.5 %copy-start.10 = (s32[128]{0:T(128)S(1)}, s32[128]{0:T(128)}, u32[]{:S(2)}) copy-start(s32[128]{0:T(128)} %param.13) | copy-start | bytes 1540
  16.0 48.4 %all-to-all-start.1 = ((f32[16,32,1536]{2,1,0:T(8,128)}), f32[16,32,1536]{2,1,0:T(8,128)}, u32[]{:S(2)}, u32[]{:S(2)}) async-start(f32[16,32,1536]{2,1,0:T(8,128)} %broadcast_select_fusion.1), calls=%async_computation.1 | async-start | bytes 6291456 | tf_op jit(solution)/shard_map/all_to_all | solution.py:142
  64.4 58.8 %all-to-all-start.3 = ((bf16[16,80,1536]{2,1,0:T(8,128)(2,1)}), bf16[16,80,1536]{2,1,0:T(8,128)(2,1)}, u32[]{:S(2)}, u32[]{:S(2)}) async-start(bf16[16,80,1536]{2,1,0:T(8,128)(2,1)} %bitcast.91), calls=%async_computation.3 | async-start | bytes 7864320 | tf_op jit(solution)/shard_map/all_to_all | solution.py:37
  123.3 143.4 %all-to-all-start = ((f32[16,32,4096]{2,1,0:T(8,128)}), f32[16,32,4096]{2,1,0:T(8,128)}, u32[]{:S(2)}, u32[]{:S(2)}) async-start(f32[16,32,4096]{2,1,0:T(8,128)} %broadcast_select_fusion), calls=%async_computation | async-start | bytes 16777216 | tf_op jit(solution)/shard_map/all_to_all | solution.py:135
  266.7 11.0 %copy-start.4 = (f32[8,32,1536]{2,1,0:T(8,128)S(1)}, f32[8,32,1536]{2,1,0:T(8,128)}, u32[]{:S(2)}) copy-start(f32[8,32,1536]{2,1,0:T(8,128)} %param.15) | copy-start | bytes 4718596
  266.7 175.5 %all-to-all-start.4 = ((bf16[16,80,4096]{2,1,0:T(8,128)(2,1)}), bf16[16,80,4096]{2,1,0:T(8,128)(2,1)}, u32[]{:S(2)}, u32[]{:S(2)}) async-start(bf16[16,80,4096]{2,1,0:T(8,128)(2,1)} %bitcast.83), calls=%async_computation.4 | async-start | bytes 20971520 | tf_op jit(solution)/shard_map/all_to_all | solution.py:36
  276.3 315.3 %reduce-scatter.2.cloned.1.call-start = ((), (), s32[]{:S(2)}) async-start(), calls=%async_computation.7 | async-start | bytes 6488064 | tf_op jit(solution)/shard_map/reduce_scatter | solution.py:64
  480.3 4.7 copy-start.6
  489.4 1.1 copy-start.2
  490.5 2.1 copy-start.3
  500.4 32.6 %all-to-all-start.2 = ((f32[16,1,22528]{2,1,0:T(1,128)}), f32[16,1,22528]{2,1,0:T(1,128)}, u32[]{:S(2)}, u32[]{:S(2)}) async-start(f32[16,1,22528]{2,1,0:T(1,128)} %copy.36), calls=%async_computation.2 | async-start | bytes 2883584 | tf_op jit(solution)/shard_map/all_to_all | solution.py:149
  532.9 28.8 %all-to-all-start.5 = ((f32[16,1,22528]{2,1,0:T(1,128)}), f32[16,1,22528]{2,1,0:T(1,128)}, u32[]{:S(2)}, u32[]{:S(2)}) async-start(f32[16,1,22528]{2,1,0:T(1,128)} %copy.44), calls=%async_computation.6 | async-start | bytes 2883584 | tf_op jit(solution)/shard_map/all_to_all | solution.py:156
  537.6 123.3 %all-gather.2.cloned.1.call-start = ((), (), s32[]{:S(2)}) async-start(), calls=%async_computation.8 | async-start | bytes 6488064 | tf_op jit(solution)/shard_map/all_gather | solution.py:88
  570.6 21.0 %copy-start.5 = (f32[1,8,32,1536]{3,1,2,0:T(8,128)S(1)}, f32[1,8,32,1536]{3,1,2,0:T(8,128)}, u32[]{:S(2)}) copy-start(f32[1,8,32,1536]{3,1,2,0:T(8,128)} %copy.54) | copy-start | bytes 4718596
  570.6 21.0 %copy-start.7 = (f32[8,22528]{1,0:T(8,128)S(1)}, f32[8,22528]{1,0:T(8,128)}, u32[]{:S(2)}) copy-start(f32[8,22528]{1,0:T(8,128)} %gather_fusion.7) | copy-start | bytes 2162692
  660.8 2.2 slice-start
  663.0 4.4 slice-start.1
  663.0 6.5 copy-start.1
Sparse Core Ops, SparseCore 0:
  489.5 102.0 reduce-scatter.1
  594.9 65.9 all-gather.1
where the time goes:
time: 684 us; the launch traced here: 677 us
  waiting for transfers between devices  429 us (63%)
  local copies, waits for them, and re-layouts  107 us (16%)
  starting transfers between devices  53.4 us (8%)
  other arithmetic  51.5 us (8%)
  matrix products  21 us (3%)
  between operations  14.4 us (2%)
    all_to_all x1, waiting for transfers between devices, route_rows(): lax.all_to_all(send_rows, 'expert', split_axis=0, concat_axis=0, tiled=True)  133 us
    all_to_all x1, waiting for transfers between devices, shards(): lax.all_to_all(outgoing(adapter_a, source_place, has_one), 'expert', spli...  114 us
    all_gather x1, waiting for transfers between devices, regather(): whole = lax.all_gather(param_share, 'dp', axis=1, tiled=True)  66.1 us
    all_to_all x1, waiting for transfers between devices, route_rows(): lax.all_to_all(send_cots, 'expert', split_axis=0, concat_axis=0, tiled=True)  34.9 us
    all_to_all x1, waiting for transfers between devices, shards(): lax.all_to_all(outgoing(adapter_b, source_place, has_one), 'expert', spli...  29.6 us
    unnamed x32, local copies, waits for them, and re-layouts  28.5 us
    all_to_all x1, waiting for transfers between devices, shards(): lax.all_to_all(outgoing(first_moment, source_place, has_one), 'expert', s...  20 us
    concatenate x4, other arithmetic, incoming(): return jnp.concatenate([local_array, received], axis=0)[pick_index]  18.2 us
  transfers between devices with their start and end apart: 8, of which 8 were waited for; matrix products, arithmetic and copies ran while one was open for 16% of the time, Pallas kernels for 0%

commit v1 on v0

v1 whole, which is shorter than its diff:
```python
import functools

import jax
import jax.numpy as jnp
from jax import lax
from jax.experimental import pallas as pl
from jax.experimental.pallas import tpu as pltpu
from jax.sharding import PartitionSpec as P

beta_one = 0.9
beta_two = 0.999
learn_rate = 0.001
decay_rate = 0.01
adam_eps = 1e-08
adapter_scale_factor = 2.0
adam_step = 10.0

D = 4096
FF = 1536
TOP = 8
R = 32
J = 8
TOK = 128
COPIES = TOK * TOP
CAP = 10
NE = 16
ND = 8
ROWS = J * CAP
RJ = R * J
UNIT = 512
SHARE = 22528
HALF = SHARE // 2
UNITS = HALF // UNIT
PIECE = HALF // 8
HC = D // 2

MESH = pl.DeviceIdType.MESH
BF = jnp.bfloat16
F32 = jnp.float32
I32 = jnp.int32


def iota(shape, dim):
    return lax.broadcasted_iota(I32, shape, dim)


def unit_place(number):
    share, inside = divmod(number, 2 * UNITS)
    half, column = divmod(inside, UNITS)
    return share, half, column


def unit_source(number):
    if number < D // UNIT * R:
        return True, number // (D // UNIT), number % (D // UNIT)
    number = number - D // UNIT * R
    return False, number // (FF // UNIT), number % (FF // UNIT)


def dispatch_kernel(
    tok, up, gate, ids_flat, ids_t, a, b, out,
    gathered, cots, send, got, ids_all, a16, b16, pick, onehot, low, weights, lows, back, grad_a, grad_b, row,
    own_sem, ids_send, ids_recv, cot_send, cot_recv, tok_send, tok_recv, sib_recv,
):
    dp = lax.axis_index("dp")
    me = lax.axis_index("expert")
    x = me // 4
    yh = (me // 2) % 2
    core = me % 2
    dp_across = (dp + 4) % 8

    def place(dy, dx, dc):
        return ((x + dx) % 4) * 4 + ((yh + dy) % 2) * 2 + (core + dc) % 2

    def device(dy, dx, dc):
        return (dp_across if dy else dp, place(dy, dx, dc))

    peers = [(dy, dx, dc) for dx in (2, 1, 3, 0) for dy in (1, 0) for dc in (0, 1) if (dy, dx, dc) != (0, 0, 0)]

    own = pltpu.make_async_copy(tok, gathered.at[pl.ds(pl.multiple_of(me * TOK, TOK), TOK)], own_sem)
    own.start()
    barrier = pltpu.get_barrier_semaphore()
    for peer in peers:
        pl.semaphore_signal(barrier, inc=1, device_id=device(*peer), device_id_type=MESH)
    pl.semaphore_wait(barrier, len(peers))
    own.wait()

    sent = []

    def block(dy, dx, dc, half, part):
        rows = place(dy, dx, dc) * TOK
        size = TOK
        if part is not None:
            rows = rows + part * (TOK // 2)
            size = TOK // 2
        return gathered.at[pl.ds(pl.multiple_of(rows, TOK // 2), size), pl.ds(half * HC, HC)]

    def push(src, half, part, to, sem):
        ref = block(*src, half, part)
        copy = pltpu.make_async_remote_copy(
            src_ref=ref, dst_ref=ref, send_sem=tok_send.at[len(sent)], recv_sem=sem, device_id=device(*to), device_id_type=MESH
        )
        copy.start()
        sent.append(copy)

    def slot(half, dy, dx, part):
        return tok_recv.at[((half * 2 + dy) * 4 + dx) * 2 + part]

    def sib_slot(half, dy, dx):
        return sib_recv.at[(half * 2 + dy) * 4 + dx]

    def arrive(half, dy, dx, part=None):
        ref = block(dy, dx, 0, half, part)
        pltpu.make_async_remote_copy(
            src_ref=ref, dst_ref=ref, send_sem=tok_send.at[0], recv_sem=slot(half, dy, dx, part or 0), device_id=device(0, 1, 0), device_id_type=MESH
        ).wait_recv()

    def to_sibling(half, dy, dx):
        push((dy, dx, 0), half, None, (0, 0, 1), sib_slot(half, dy, dx))

    def to_across(half, dx):
        push((0, dx, 0), half, None, (1, 0, 0), slot(half, 1, dx, 0))

    def to_right(half, dy, dx, part=None):
        push((dy, dx, 0), half, part, (0, 1, 0), slot(half, dy, (dx + 3) % 4, part or 0))

    def to_left(half, dy, dx, part=None):
        push((dy, dx, 0), half, part, (0, 3, 0), slot(half, dy, (dx + 1) % 4, part or 0))

    to_across(1, 0)
    to_right(0, 0, 0)
    to_left(0, 0, 0)
    to_across(0, 0)
    to_right(1, 0, 0)
    to_left(1, 0, 0)
    to_sibling(0, 0, 0)
    to_sibling(1, 0, 0)

    small = []
    mine = ids_all.at[pl.ds(pl.multiple_of(me * TOP, TOP), TOP)]
    ids_all[pl.ds(pl.multiple_of(me * TOP, TOP), TOP), :] = ids_t[...]
    for number, peer in enumerate(peers):
        copy = pltpu.make_async_remote_copy(
            src_ref=mine, dst_ref=mine, send_sem=ids_send.at[number], recv_sem=ids_recv.at[me], device_id=device(*peer), device_id_type=MESH
        )
        copy.start()
        small.append(copy)

    before = (iota((TOK, TOK), 0) < iota((TOK, TOK), 1)).astype(BF)
    experts = iota((TOK, TOK), 0)
    total = jnp.zeros((TOK, 1), F32)
    for part in range(TOP):
        hit = ids_flat[:, part * TOK:(part + 1) * TOK] == experts
        value = hit.astype(F32)
        count = jnp.dot(value.astype(BF), before, preferred_element_type=F32) + total
        total = total + jnp.sum(value, axis=1, keepdims=True)
        row[:, part * TOK:(part + 1) * TOK] = jnp.sum(
            jnp.where(hit, count + (CAP * experts).astype(F32), 0.0), axis=0, keepdims=True
        ).astype(I32)

    @pl.loop(0, TOP)
    def _(part):
        rows = pl.ds(pl.multiple_of(part * TOK, TOK), TOK)
        cots[rows, :] = (gate[rows, :] * up[rows, :].astype(F32)).astype(BF)

    def pack(dx):
        base = pl.multiple_of(((x + dx) % 4) * (4 * ROWS), 4 * ROWS)
        pick[...] = jnp.where(iota((4 * ROWS, COPIES), 0) + base == row[...], 1.0, 0.0).astype(BF)

        @pl.loop(0, FF // UNIT)
        def _(part):
            cols = pl.ds(pl.multiple_of(part * UNIT, UNIT), UNIT)
            send[pl.ds(base, 4 * ROWS), cols] = jnp.dot(pick[...], cots[:, cols], preferred_element_type=F32).astype(BF)

    cot_sent = []
    for dx in (2, 1, 3, 0):
        pack(dx)
        for peer in [p for p in peers if p[1] == dx]:
            copy = pltpu.make_async_remote_copy(
                src_ref=send.at[pl.ds(pl.multiple_of(place(*peer) * ROWS, ROWS), ROWS)],
                dst_ref=got.at[pl.ds(pl.multiple_of(me * ROWS, ROWS), ROWS)],
                send_sem=cot_send.at[len(cot_sent)], recv_sem=cot_recv.at[me],
                device_id=device(*peer), device_id_type=MESH,
            )
            copy.start()
            cot_sent.append(copy)
    my_rows = pl.ds(pl.multiple_of(me * ROWS, ROWS), ROWS)
    got[my_rows, :] = send[my_rows, :]

    arrive(1, 1, 0)
    to_right(1, 1, 0)
    to_left(1, 1, 0)
    to_sibling(1, 1, 0)
    arrive(0, 0, 3)
    to_right(0, 0, 3, 0)
    to_across(0, 3)
    to_sibling(0, 0, 3)
    arrive(0, 0, 1)
    to_left(0, 0, 1, 1)
    to_across(0, 1)
    to_sibling(0, 0, 1)
    arrive(0, 1, 0)
    to_sibling(0, 1, 0)
    arrive(1, 0, 3)
    to_right(1, 0, 3, 0)
    to_sibling(1, 0, 3)
    arrive(1, 0, 1)
    to_left(1, 0, 1, 1)
    to_sibling(1, 0, 1)
    arrive(0, 0, 2, 0)
    arrive(0, 0, 2, 1)
    to_across(0, 2)
    to_sibling(0, 0, 2)
    arrive(1, 1, 3)
    to_right(1, 1, 3, 0)
    to_sibling(1, 1, 3)
    arrive(1, 1, 1)
    to_left(1, 1, 1, 1)
    to_sibling(1, 1, 1)
    arrive(0, 1, 3)
    to_sibling(0, 1, 3)
    arrive(0, 1, 1)
    to_sibling(0, 1, 1)

    turn = (iota((RJ, RJ), 1) == (iota((RJ, RJ), 0) % J) * R + iota((RJ, RJ), 0) // J).astype(F32).astype(BF)

    @pl.loop(0, D // UNIT)
    def _(part):
        cols = pl.ds(pl.multiple_of(part * UNIT, UNIT), UNIT)
        a16[:, cols] = jnp.dot(turn, a[:, cols].astype(BF), preferred_element_type=F32).astype(BF)

    @pl.loop(0, FF // UNIT)
    def _(part):
        cols = pl.ds(pl.multiple_of(part * UNIT, UNIT), UNIT)
        b16[:, cols] = jnp.dot(turn, b[:, cols].astype(BF), preferred_element_type=F32).astype(BF)

    for peer in peers:
        ref = ids_all.at[pl.ds(pl.multiple_of(place(*peer) * TOP, TOP), TOP)]
        pltpu.make_async_remote_copy(
            src_ref=ref, dst_ref=ref, send_sem=ids_send.at[0], recv_sem=ids_recv.at[place(*peer)], device_id=device(*peer), device_id_type=MESH
        ).wait_recv()
    repeat = (iota((ROWS, J), 0) // CAP == iota((ROWS, J), 1)).astype(F32).astype(BF)
    turn_in = (iota((ROWS, TOK), 0) % CAP).astype(F32)

    @pl.loop(0, NE)
    def _(source):
        ids = ids_all[pl.ds(pl.multiple_of(source * TOP, TOP), TOP), :]
        hit = jnp.zeros((J, TOK), F32)
        for k in range(TOP):
            hit = hit + jnp.where(ids[k:k + 1, :] == iota((J, TOK), 0) + me * J, 1.0, 0.0)
        count = jnp.dot(hit.astype(BF), before, preferred_element_type=F32)
        value = jnp.where(hit > 0.5, count, -1.0)
        spread = jnp.dot(repeat, value.astype(BF), preferred_element_type=F32)
        onehot[pl.ds(pl.multiple_of(source * ROWS, ROWS), ROWS), :] = jnp.where(spread == turn_in, 1.0, 0.0).astype(BF)

    for peer in peers:
        ref = got.at[pl.ds(pl.multiple_of(place(*peer) * ROWS, ROWS), ROWS)]
        pltpu.make_async_remote_copy(
            src_ref=ref, dst_ref=ref, send_sem=cot_send.at[0], recv_sem=cot_recv.at[place(*peer)], device_id=device(*peer), device_id_type=MESH
        ).wait_recv()

    own_column = (iota((4 * ROWS, RJ), 0) % ROWS) // CAP == iota((4 * ROWS, RJ), 1) % J

    @pl.loop(0, 4)
    def _(part):
        rows = pl.ds(pl.multiple_of(part * (4 * ROWS), 4 * ROWS), 4 * ROWS)
        value = lax.dot_general(got[rows, :], b16[...], (((1,), (1,)), ((), ())), preferred_element_type=F32)
        back[rows, :] = jnp.where(own_column, value, 0.0).astype(BF)

    @pl.loop(0, NE)
    def _(source):
        rows = pl.ds(pl.multiple_of(source * ROWS, ROWS), ROWS)
        cols = pl.ds(pl.multiple_of(source * TOK, TOK), TOK)
        weights[:, cols] = lax.dot_general(
            back[rows, :], onehot[rows, :], (((0,), (0,)), ((), ())), preferred_element_type=F32
        ).astype(BF)

    arrive(1, 0, 2, 0)
    arrive(1, 0, 2, 1)
    to_sibling(1, 0, 2)
    arrive(1, 1, 2, 0)
    arrive(1, 1, 2, 1)
    to_sibling(1, 1, 2)
    arrive(0, 1, 2)
    to_sibling(0, 1, 2)
    for half in range(2):
        for dy in range(2):
            for dx in range(4):
                ref = block(dy, dx, 1, half, None)
                pltpu.make_async_remote_copy(
                    src_ref=ref, dst_ref=ref, send_sem=tok_send.at[0], recv_sem=sib_slot(half, dy, dx), device_id=device(0, 0, 1), device_id_type=MESH
                ).wait_recv()

    @pl.loop(0, 4)
    def _(part):
        rows = pl.ds(pl.multiple_of(part * UNIT, UNIT), UNIT)
        low[rows, :] = lax.dot_general(
            gathered[rows, :], a16[...], (((1,), (1,)), ((), ())), preferred_element_type=F32
        ).astype(BF)

    @pl.loop(0, NE)
    def _(source):
        rows = pl.ds(pl.multiple_of(source * ROWS, ROWS), ROWS)
        value = jnp.dot(onehot[rows, :], low[pl.ds(pl.multiple_of(source * TOK, TOK), TOK), :], preferred_element_type=F32)
        lows[rows, :] = jnp.where(own_column[:ROWS], value, 0.0).astype(BF)

    @pl.loop(0, D // UNIT)
    def _(part):
        cols = pl.ds(pl.multiple_of(part * UNIT, UNIT), UNIT)
        grad_a[:, cols] = jnp.dot(weights[...], gathered[:, cols], preferred_element_type=F32)

    @pl.loop(0, FF // UNIT)
    def _(part):
        cols = pl.ds(pl.multiple_of(part * UNIT, UNIT), UNIT)
        grad_b[:, cols] = lax.dot_general(lows[...], got[:, cols], (((0,), (0,)), ((), ())), preferred_element_type=F32)

    def grad_unit(number):
        from_a, r, column = unit_source(number)
        ref = grad_a if from_a else grad_b
        return ref[r * J:(r + 1) * J, column * UNIT:(column + 1) * UNIT]

    for share in range(ND):
        for column in range(UNITS):
            first = share * 2 * UNITS + column
            both = jnp.concatenate([grad_unit(first), grad_unit(first + UNITS)], axis=0)
            out[share * 16:(share + 1) * 16, column * UNIT:(column + 1) * UNIT] = both.astype(BF)

    for copy in sent + small + cot_sent:
        copy.wait_send()


def update_kernel(
    grads, a, b, first, second, meta, whole, first_out, second_out,
    got, shared, rows_a, rows_b, param, moving, packed, landed,
    grad_send, grad_recv, move_send, move_recv, all_send, all_recv, own_sem,
):
    dp = lax.axis_index("dp")
    me = lax.axis_index("expert")
    barrier = pltpu.get_barrier_semaphore()
    groups = [((dp + step) % ND, me) for step in range(1, ND)]
    homes = [(dp, (me + step) % NE) for step in range(1, NE)]
    for peer in groups + homes:
        pl.semaphore_signal(barrier, inc=1, device_id=peer, device_id_type=MESH)
    pl.semaphore_wait(barrier, len(groups) + len(homes))

    def rows16(index):
        return pl.ds(pl.multiple_of(index * 16, 16), 16)

    grad_sent = []
    for step in (4, 1, 7, 3, 5, 2, 6):
        to = groups[step - 1]
        copy = pltpu.make_async_remote_copy(
            src_ref=grads.at[rows16(to[0])], dst_ref=got.at[rows16(dp)], send_sem=grad_send.at[step], recv_sem=grad_recv.at[dp],
            device_id=to, device_id_type=MESH,
        )
        copy.start()
        grad_sent.append(copy)
    got[rows16(dp), :] = grads[rows16(dp), :]

    exact = lax.Precision.HIGHEST
    start = 2 * UNITS * dp
    a_first = jnp.minimum(start // (D // UNIT), R - 8)
    b_first = jnp.clip((start - D // UNIT * R) // (FF // UNIT), 0, R - 16)

    def chooser(count, base):
        index = iota((count * J, RJ), 0)
        return (iota((count * J, RJ), 1) == (index % J) * R + index // J + base).astype(F32)

    @pl.loop(0, D // UNIT)
    def _(part):
        cols = pl.ds(pl.multiple_of(part * UNIT, UNIT), UNIT)
        rows_a[:, cols] = jnp.dot(chooser(8, a_first), a[:, cols], preferred_element_type=F32, precision=exact)

    @pl.loop(0, FF // UNIT)
    def _(part):
        cols = pl.ds(pl.multiple_of(part * UNIT, UNIT), UNIT)
        rows_b[:, cols] = jnp.dot(chooser(16, b_first), b[:, cols], preferred_element_type=F32, precision=exact)

    @pl.loop(0, UNITS)
    def _(column):
        for half in range(2):
            number = start + half * UNITS + column
            in_a = jnp.clip(number // (D // UNIT) - a_first, 0, 7)
            col_a = number % (D // UNIT)
            number_b = jnp.maximum(number - D // UNIT * R, 0)
            in_b = jnp.clip(number_b // (FF // UNIT) - b_first, 0, 15)
            col_b = number_b % (FF // UNIT)
            value_a = rows_a[pl.ds(pl.multiple_of(in_a * J, J), J), pl.ds(pl.multiple_of(col_a * UNIT, UNIT), UNIT)]
            value_b = rows_b[pl.ds(pl.multiple_of(in_b * J, J), J), pl.ds(pl.multiple_of(col_b * UNIT, UNIT), UNIT)]
            param[half * J:(half + 1) * J, pl.ds(pl.multiple_of(column * UNIT, UNIT), UNIT)] = jnp.where(
                number < D // UNIT * R, value_a, value_b
            )

    index = iota((256, 128), 0)
    lane = iota((256, 128), 1)
    same = (index % 8 == lane // 16) & ((index // 8) % 2 == (lane // 8) % 2)
    leave = (same & (index // 16 == meta[0:1, :]) & (index // 16 != me)).astype(F32).astype(BF)
    enter = (same & (index // 16 == meta[1:2, :]) & (index // 16 != me)).astype(F32).astype(BF)
    index = iota((128, 128), 0)
    lane = iota((128, 128), 1)
    stay = ((index // 8 == lane // 8) & (index % 8 == meta[2:3, :]) & (meta[1:2, :] == me)).astype(F32).astype(BF)

    for step in range(1, ND):
        ref = got.at[rows16((dp + step) % ND)]
        pltpu.make_async_remote_copy(
            src_ref=ref, dst_ref=ref, send_sem=grad_send.at[0], recv_sem=grad_recv.at[(dp + step) % ND],
            device_id=groups[step - 1], device_id_type=MESH,
        ).wait_recv()

    fix_one = 1.0 - beta_one**adam_step
    fix_two = 1.0 - beta_two**adam_step

    @pl.loop(0, 8)
    def _(piece):
        cols = pl.ds(pl.multiple_of(piece * PIECE, 128), PIECE)
        late = pl.ds(pl.multiple_of(HALF + piece * PIECE, 128), PIECE)
        grad = got[0:16, cols].astype(F32)
        for source in range(1, ND):
            grad = grad + got[source * 16:(source + 1) * 16, cols].astype(F32)
        grad = adapter_scale_factor * grad
        one = beta_one * jnp.concatenate([first[:, cols], first[:, late]], axis=0) + (1.0 - beta_one) * grad
        two = beta_two * jnp.concatenate([second[:, cols], second[:, late]], axis=0) + (1.0 - beta_two) * grad * grad
        old = param[:, cols]
        new = old - learn_rate * (one / fix_one / (jnp.sqrt(two / fix_two) + adam_eps) + decay_rate * old)
        place = rows16(piece)
        moving[0, place, :] = new.astype(BF)
        moving[1, place, :] = one.astype(BF)
        moving[2, place, :] = two.astype(BF)

    move_sent = []
    for kind in range(3):
        packed[kind] = jnp.dot(leave, moving[kind], preferred_element_type=F32).astype(BF)
        landed[kind, rows16(me), :] = jnp.zeros((16, PIECE), BF)
        for step in (8, 9, 10, 11, 7, 6, 5, 4, 12, 13, 14, 15, 3, 2, 1):
            to = homes[step - 1]
            copy = pltpu.make_async_remote_copy(
                src_ref=packed.at[kind, rows16(to[1])], dst_ref=landed.at[kind, rows16(me)],
                send_sem=move_send.at[kind * NE + step], recv_sem=move_recv.at[kind * NE + me],
                device_id=to, device_id_type=MESH,
            )
            copy.start()
            move_sent.append(copy)

    def arrived(kind):
        for step in range(1, NE):
            source = (me + step) % NE
            ref = landed.at[kind, rows16(source)]
            pltpu.make_async_remote_copy(
                src_ref=ref, dst_ref=ref, send_sem=move_send.at[0], recv_sem=move_recv.at[kind * NE + source],
                device_id=homes[step - 1], device_id_type=MESH,
            ).wait_recv()
        took = (((0,), (0,)), ((), ()))
        return lax.dot_general(enter, landed[kind], took, preferred_element_type=F32) + lax.dot_general(
            stay, moving[kind], took, preferred_element_type=F32
        )

    new = arrived(0).astype(BF)
    for piece in range(8):
        shared[:, piece * PIECE:(piece + 1) * PIECE] = new[piece * 16:(piece + 1) * 16, :]
    all_sent = []
    for step in (4, 1, 7, 3, 5, 2, 6):
        copy = pltpu.make_async_remote_copy(
            src_ref=shared, dst_ref=whole.at[rows16(dp)], send_sem=all_send.at[step], recv_sem=all_recv.at[dp],
            device_id=groups[step - 1], device_id_type=MESH,
        )
        copy.start()
        all_sent.append(copy)
    keep = pltpu.make_async_copy(shared, whole.at[rows16(dp)], own_sem)
    keep.start()
    first_out[...] = arrived(1).astype(BF)
    second_out[...] = arrived(2).astype(BF)
    for step in range(1, ND):
        ref = whole.at[rows16((dp + step) % ND)]
        pltpu.make_async_remote_copy(
            src_ref=ref, dst_ref=ref, send_sem=all_send.at[0], recv_sem=all_recv.at[(dp + step) % ND],
            device_id=groups[step - 1], device_id_type=MESH,
        ).wait_recv()
    keep.wait()
    for copy in grad_sent + move_sent + all_sent:
        copy.wait_send()


def finish_kernel(whole, first, second, new_a, new_b, new_first, new_second):
    turn = (iota((RJ, RJ), 1) == (iota((RJ, RJ), 0) % R) * J + iota((RJ, RJ), 0) // R).astype(F32).astype(BF)

    def unit(number):
        share, half, column = unit_place(number)
        value = whole[share * 16:(share + 1) * 16, column * UNIT:(column + 1) * UNIT].astype(F32)
        return value[half * J:(half + 1) * J]

    for out, columns, base in ((new_a, D // UNIT, 0), (new_b, FF // UNIT, D // UNIT * R)):
        for column in range(columns):
            stack = jnp.concatenate([unit(base + r * columns + column) for r in range(R)], axis=0).astype(BF)
            out[:, column * UNIT:(column + 1) * UNIT] = jnp.dot(turn, stack, preferred_element_type=F32)
    for out, value in ((new_first, first), (new_second, second)):
        for piece in range(8):
            both = value[piece * 16:(piece + 1) * 16, :].astype(F32)
            out[:, piece * PIECE:(piece + 1) * PIECE] = both[:J]
            out[:, HALF + piece * PIECE:HALF + (piece + 1) * PIECE] = both[J:]


def vmem(count):
    return [pl.BlockSpec(memory_space=pltpu.VMEM)] * count


def shards(tokens, up_grad, gate_weights, expert_ids, new_home, adapter_a, adapter_b, first_moment, second_moment):
    me = lax.axis_index("expert")
    places = jnp.arange(J, dtype=I32)
    dest = lax.dynamic_slice_in_dim(new_home, me * J, J, 0) // J
    named = new_home[None, :] == (me * J + places)[:, None]
    owner = jnp.sum(jnp.where(named, jnp.arange(NE * J, dtype=I32)[None, :], 0), axis=1)
    meta = jnp.tile(jnp.stack([dest, owner // J, owner % J] + [places] * 5), (1, 16))
    a = adapter_a.reshape(RJ, D)
    b = adapter_b.reshape(RJ, FF)
    dma = pltpu.SemaphoreType.DMA
    grads = pl.pallas_call(
        dispatch_kernel,
        out_shape=jax.ShapeDtypeStruct((ND * 16, HALF), BF),
        in_specs=[pl.BlockSpec(memory_space=pl.ANY)] + vmem(6),
        out_specs=pl.BlockSpec(memory_space=pltpu.VMEM),
        scratch_shapes=[
            pltpu.VMEM((NE * TOK, D), BF),
            pltpu.VMEM((COPIES, FF), BF),
            pltpu.VMEM((NE * ROWS, FF), BF),
            pltpu.VMEM((NE * ROWS, FF), BF),
            pltpu.VMEM((NE * TOP, TOK), I32),
            pltpu.VMEM((RJ, D), BF),
            pltpu.VMEM((RJ, FF), BF),
            pltpu.VMEM((4 * ROWS, COPIES), BF),
            pltpu.VMEM((NE * ROWS, TOK), BF),
            pltpu.VMEM((NE * TOK, RJ), BF),
            pltpu.VMEM((RJ, NE * TOK), BF),
            pltpu.VMEM((NE * ROWS, RJ), BF),
            pltpu.VMEM((NE * ROWS, RJ), BF),
            pltpu.VMEM((RJ, D), F32),
            pltpu.VMEM((RJ, FF), F32),
            pltpu.VMEM((1, COPIES), I32),
            dma,
            dma((NE,)),
            dma((NE,)),
            dma((NE,)),
            dma((NE,)),
            dma((64,)),
            dma((32,)),
            dma((16,)),
        ],
        compiler_params=pltpu.CompilerParams(collective_id=0, has_side_effects=True, vmem_limit_bytes=60 * 2**20),
        name="dispatch",
    )(
        tokens, up_grad.reshape(COPIES, FF), gate_weights.reshape(COPIES, 1), expert_ids.reshape(1, COPIES), expert_ids.T, a, b,
    )
    whole, first, second = pl.pallas_call(
        update_kernel,
        out_shape=[
            jax.ShapeDtypeStruct((ND * 16, HALF), BF),
            jax.ShapeDtypeStruct((128, PIECE), BF),
            jax.ShapeDtypeStruct((128, PIECE), BF),
        ],
        in_specs=vmem(6),
        out_specs=vmem(3),
        scratch_shapes=[
            pltpu.VMEM((ND * 16, HALF), BF),
            pltpu.VMEM((16, HALF), BF),
            pltpu.VMEM((8 * J, D), F32),
            pltpu.VMEM((16 * J, FF), F32),
            pltpu.VMEM((16, HALF), F32),
            pltpu.VMEM((3, 128, PIECE), BF),
            pltpu.VMEM((3, 256, PIECE), BF),
            pltpu.VMEM((3, 256, PIECE), BF),
            dma((ND,)),
            dma((ND,)),
            dma((3 * NE,)),
            dma((3 * NE,)),
            dma((ND,)),
            dma((ND,)),
            dma,
        ],
        compiler_params=pltpu.CompilerParams(collective_id=1, has_side_effects=True, vmem_limit_bytes=60 * 2**20),
        name="update",
    )(grads, a, b, first_moment, second_moment, meta)
    new_a, new_b, new_first, new_second = pl.pallas_call(
        finish_kernel,
        out_shape=[
            jax.ShapeDtypeStruct((RJ, D), F32),
            jax.ShapeDtypeStruct((RJ, FF), F32),
            jax.ShapeDtypeStruct((J, SHARE), F32),
            jax.ShapeDtypeStruct((J, SHARE), F32),
        ],
        in_specs=vmem(3),
        out_specs=vmem(4),
        compiler_params=pltpu.CompilerParams(vmem_limit_bytes=60 * 2**20),
        name="finish",
    )(whole, first, second)
    return new_a.reshape(J, R, D), new_b.reshape(J, R, FF), new_first, new_second


def solution(mesh):
    placed = (
        P(("dp", "expert"), None),
        P(("dp", "expert"), None, None),
        P(("dp", "expert"), None),
        P(("dp", "expert"), None),
        P(),
        P("expert", None, None),
        P("expert", None, None),
        P("expert", "dp"),
        P("expert", "dp"),
    )
    return jax.shard_map(
        shards,
        mesh=mesh,
        in_specs=placed,
        out_specs=(P("expert", None, None), P("expert", None, None), P("expert", "dp"), P("expert", "dp")),
        check_vma=False,
    )
```

time: 684 us -> 259 us (0.38)
  waiting for transfers between devices: 429 us -> 0 us
  Pallas kernels: 0 us -> 252 us
  local copies, waits for them, and re-layouts: 107 us -> 3.97 us
  starting transfers between devices: 53.4 us -> 0 us
  other arithmetic: 51.5 us -> 1.59 us
  matrix products: 21 us -> 0 us
  between operations: 14.4 us -> 0.67 us
    all_to_all x6 -> x0, waiting for transfers between devices: 349 us -> none  [the longest x1 133 us: route_rows(): lax.all_to_all(send_rows, 'expert', split_axis=0, concat_axis=0, tiled=True)]
    pallas_call x0 -> x3, Pallas kernels: none -> 252 us  [the longest x1 139 us: shards(): pl.pallas_call(dispatch_kernel, out_shape=jax.ShapeDtypeStruct((ND * 16,...]
    all_gather x1 -> x0, waiting for transfers between devices: 66.1 us -> none  [regather(): whole = lax.all_gather(param_share, 'dp', axis=1, tiled=True)]
    all_to_all x6 -> x0, starting transfers between devices: 53.3 us -> none  [the longest x1 12.5 us: shards(): lax.all_to_all(outgoing(adapter_a, source_place, has_one), 'expert', spli...]
    gather x8 -> x0, local copies, waits for them, and re-layouts: 31.1 us -> none  [the longest x4 16.6 us: incoming(): return jnp.concatenate([local_array, received], axis=0)[pick_index]]
    unnamed x32 -> x2, local copies, waits for them, and re-layouts: 28.5 us -> 1.57 us
    concatenate x5 -> x0, other arithmetic: 22.6 us -> none  [the longest x4 18.2 us: incoming(): return jnp.concatenate([local_array, received], axis=0)[pick_index]]
    dot_general x2 -> x0, matrix products: 21 us -> none  [the longest x1 11.2 us: group_gradients(): jnp.einsum('pjcr,pjcf->jrf', low_rank_hidden, got_cots, preferred_element...]
  transfers between devices with their start and end apart: 8 -> 0, of which waited for: 8 -> 0; matrix products, arithmetic and copies ran while one was open for 16% -> 0% of each run, Pallas kernels for 0% -> 0%
where the time goes in v1:
time: 259 us; the launch traced here: 258 us
  Pallas kernels  252 us (97%)
  local copies, waits for them, and re-layouts  3.97 us (2%)
    pallas_call x1, Pallas kernels, shards(): pl.pallas_call(dispatch_kernel, out_shape=jax.ShapeDtypeStruct((ND * 16,...  139 us
    pallas_call x1, Pallas kernels, shards(): pl.pallas_call(update_kernel, out_shape=[jax.ShapeDtypeStruct((ND * 16, H...  108 us
    pallas_call x1, Pallas kernels, shards(): pl.pallas_call(finish_kernel, out_shape=[jax.ShapeDtypeStruct((RJ, D), F3...  5.61 us

profile of v1, /device:TPU:1, one launch (start us, length us, event | category | flops | bytes accessed | tf_op | source)
XLA Modules:
  0.0 258.2 jit_solution(6648743071601976633)
XLA Ops:
  0.6 0.7 fusion
  1.4 0.8 select_reduce_fusion
  2.3 0.7 tile.10.meta
  3.0 0.8 copy.18
  3.7 0.8 copy.19
  4.5 0.7 reshape.112.ids_flat
  5.2 1.0 reshape.117.gate
  6.2 138.7 %dispatch.1.grads = bf16[128,11264]{1,0:T(8,128)(2,1)} custom-call(bf16[128,4096]{1,0:T(8,128)(2,1)} %tok.1, bf16[1024,1536]{1,0:T(8,128)(2,1)} %bitcast.27, f32[1024,1]{1,0:T(8,128)} %reshape.117.gate, s32[1,1024]{1,0:T(1,128)} %reshape.112.ids_flat, s32[8,128]{1,0:T(8,128)} %bitcast.28, f32[256,4096]{1,0:T(8,128)} %bitcast.23, f32[256,1536]{1,0:T(8,128)} %bitcast.25), custom_call_target="tpu_custom_call" | custom-call | tf_op jit(solution)/shard_map/dispatch/pallas_call | solution.py:516
  144.9 107.7 %update.1 = (bf16[128,11264]{1,0:T(8,128)(2,1)}, bf16[128,1408]{1,0:T(8,128)(2,1)}, bf16[128,1408]{1,0:T(8,128)(2,1)}) custom-call(bf16[128,11264]{1,0:T(8,128)(2,1)} %dispatch.1.grads, f32[256,4096]{1,0:T(8,128)} %bitcast.24, f32[256,1536]{1,0:T(8,128)} %bitcast.26, f32[8,22528]{1,0:T(8,128)} %first.1, f32[8,22528]{1,0:T(8,128)} %second.1, s32[8,128]{1,0:T(8,128)} %tile.10.meta), custom_call_target="tpu_custom_call" | custom-call | tf_op jit(solution)/shard_map/update/pallas_call | solution.py:552
  252.6 5.6 %finish.1 = (f32[256,4096]{1,0:T(8,128)}, f32[256,1536]{1,0:T(8,128)}, f32[8,22528]{1,0:T(8,128)}, f32[8,22528]{1,0:T(8,128)}) custom-call(bf16[128,11264]{1,0:T(8,128)(2,1)} %get-tuple-element.11.whole, bf16[128,1408]{1,0:T(8,128)(2,1)} %get-tuple-element.12.first, bf16[128,1408]{1,0:T(8,128)(2,1)} %get-tuple-element.13.second), custom_call_target="tpu_custom_call" | custom-call | tf_op jit(solution)/shard_map/finish/pallas_call | solution.py:581
  (5 shorter events, 0.1 us)

commit v2 on v1

v2 whole, which is shorter than its diff:
```python
import jax
import jax.numpy as jnp
from jax import lax
from jax.experimental import pallas as pl
from jax.experimental.pallas import tpu as pltpu
from jax.sharding import PartitionSpec as P

beta_one = 0.9
beta_two = 0.999
learn_rate = 0.001
decay_rate = 0.01
adam_eps = 1e-08
adapter_scale_factor = 2.0
adam_step = 10.0

D = 4096
FF = 1536
TOP = 8
R = 32
J = 8
TOK = 128
COPIES = TOK * TOP
CAP = 10
NE = 16
ND = 8
ROWS = J * CAP
EARLY = 48
LATE = ROWS - EARLY
RJ = R * J
CH = 4
RC = R * CH
UNIT = 512
SHARE = 22528
PIECE = SHARE // 16
QUARTER = SHARE // 4
UNITS = QUARTER // UNIT
A_UNITS = D // UNIT
B_UNITS = FF // UNIT
SPLIT = 1536
Y_FIRST = 48

MESH = pl.DeviceIdType.MESH
BF = jnp.bfloat16
F32 = jnp.float32
I32 = jnp.int32


def iota(shape, dim):
    return lax.broadcasted_iota(I32, shape, dim)


def ones(mask):
    return mask.astype(F32).astype(BF)


def contract(lhs, rhs, i, k, precision=None):
    return lax.dot_general(lhs, rhs, (((i,), (k,)), ((), ())), preferred_element_type=F32, precision=precision)


def at(start, size, unit=None):
    return pl.ds(pl.multiple_of(start, unit or size), size)


def main_kernel(
    tok, up_hbm, gate_t, ids_t, homes_row, a_hbm, b_hbm, first_hbm, second_hbm, whole, first_out, second_out,
    gathered, cots, send, got_early, got_late, ids_all, a, b, a16, b16, pick, hot_early, hot_late, low, weights,
    low_early, low_late, back_early, back_late, grad_a, grad_b, row, wire, wire_got,
    first, second, rows_a, rows_b, param, moving, packed, landed,
    local, ids_send, ids_recv, cot_send, cot_recv, tok_send, tok_recv, sib_recv,
    grad_send, grad_recv, move_send, move_recv, all_send, all_recv,
):
    dp = lax.axis_index("dp")
    me = lax.axis_index("expert")
    x = me // 4
    yh = (me // 2) % 2
    core = me % 2
    dp_across = (dp + 4) % 8
    yl = dp // 4
    z = dp % 4

    def place(dy, dx, dc):
        return ((x + dx) % 4) * 4 + ((yh + dy) % 2) * 2 + (core + dc) % 2

    def device(dy, dx, dc):
        return (dp_across if dy else dp, place(dy, dx, dc))

    def copy_to(src, dst, send_sem, recv_sem, to):
        return pltpu.make_async_remote_copy(
            src_ref=src, dst_ref=dst, send_sem=send_sem, recv_sem=recv_sem, device_id=to, device_id_type=MESH
        )

    peers = [
        (1, 0, 0), (0, 2, 0), (0, 1, 0), (0, 3, 0), (1, 2, 0), (1, 0, 1), (0, 2, 1), (1, 1, 0),
        (0, 3, 1), (1, 2, 1), (1, 3, 0), (0, 1, 1), (1, 1, 1), (1, 3, 1), (0, 0, 1),
    ]
    groups = [((dp + step) % ND, me) for step in range(1, ND)]
    homes = [(dp, (me + step) % NE) for step in range(1, NE)]

    loads = [
        pltpu.make_async_copy(src, dst, local.at[number])
        for number, (src, dst) in enumerate([
            (tok, gathered.at[at(me * TOK, TOK)]), (up_hbm, cots), (a_hbm, a), (b_hbm, b), (first_hbm, first), (second_hbm, second),
        ])
    ]
    for load in loads:
        load.start()
    barrier = pltpu.get_barrier_semaphore()
    met = groups + homes + [device(*peer) for peer in peers if peer[0]]
    for peer in met:
        pl.semaphore_signal(barrier, inc=1, device_id=peer, device_id_type=MESH)
    pl.semaphore_wait(barrier, len(met))
    loads[0].wait()

    sent = []

    def block(dy, dx, dc, half, part):
        rows = place(dy, dx, dc) * TOK
        size = TOK
        if part is not None:
            rows = rows + part * (TOK // 2)
            size = TOK // 2
        cols = pl.ds(SPLIT, D - SPLIT) if half else pl.ds(0, SPLIT)
        return gathered.at[at(rows, size), cols]

    def push(src, half, part, to, sem):
        ref = block(*src, half, part)
        copy = copy_to(ref, ref, tok_send.at[len(sent)], sem, device(*to))
        copy.start()
        sent.append(copy)

    def slot(half, dy, dx, part):
        return tok_recv.at[((half * 2 + dy) * 4 + dx) * 2 + part]

    def sib_slot(half, dy, dx):
        return sib_recv.at[(half * 2 + dy) * 4 + dx]

    def arrive(half, dy, dx, part=None):
        ref = block(dy, dx, 0, half, part)
        copy_to(ref, ref, tok_send.at[0], slot(half, dy, dx, part or 0), device(0, 1, 0)).wait_recv()

    def to_sibling(half, dy, dx):
        push((dy, dx, 0), half, None, (0, 0, 1), sib_slot(half, dy, dx))

    def to_across(half, dx):
        push((0, dx, 0), half, None, (1, 0, 0), slot(half, 1, dx, 0))

    def to_right(half, dy, dx, part=None):
        push((dy, dx, 0), half, part, (0, 1, 0), slot(half, dy, (dx + 3) % 4, part or 0))

    def to_left(half, dy, dx, part=None):
        push((dy, dx, 0), half, part, (0, 3, 0), slot(half, dy, (dx + 1) % 4, part or 0))

    to_across(1, 0)
    to_right(0, 0, 0)
    to_left(0, 0, 0)
    to_across(0, 0)
    to_right(1, 0, 0)
    to_left(1, 0, 0)
    to_sibling(0, 0, 0)
    to_sibling(1, 0, 0)

    small = []
    mine = at(me * TOP, TOP)
    ids_all[mine, :] = ids_t[...]
    for number, peer in enumerate(peers):
        copy = copy_to(ids_all.at[mine], ids_all.at[mine], ids_send.at[number], ids_recv.at[me], device(*peer))
        copy.start()
        small.append(copy)

    owner_of = iota((TOK, COPIES), 1) // TOP == iota((TOK, COPIES), 0)
    which = iota((TOP, COPIES), 1) % TOP == iota((TOP, COPIES), 0)
    spread = jnp.dot(ids_t[...].astype(F32).astype(BF), ones(owner_of), preferred_element_type=F32)
    ids_flat = jnp.sum(jnp.where(which, spread, 0.0), axis=0, keepdims=True).astype(I32)
    before = ones(iota((TOK, TOK), 0) < iota((TOK, TOK), 1))
    experts = iota((TOK, TOK), 0)
    total = jnp.zeros((TOK, 1), F32)
    for part in range(TOP):
        hit = ids_flat[:, part * TOK:(part + 1) * TOK] == experts
        value = hit.astype(F32)
        count = jnp.dot(value.astype(BF), before, preferred_element_type=F32) + total
        total = total + jnp.sum(value, axis=1, keepdims=True)
        row[:, part * TOK:(part + 1) * TOK] = jnp.sum(
            jnp.where(hit, count + (CAP * experts).astype(F32), 0.0), axis=0, keepdims=True
        ).astype(I32)

    loads[1].wait()

    @pl.loop(0, TOP)
    def _(part):
        rows = at(part * TOK, TOK)
        mine_of = (iota((TOK, TOK), 0) + part * TOK) // TOP == iota((TOK, TOK), 1)
        scale = contract(mine_of.astype(F32), gate_t[...], 1, 1, lax.Precision.HIGHEST)
        scale = jnp.sum(jnp.where(iota((TOK, TOP), 0) % TOP == iota((TOK, TOP), 1), scale, 0.0), axis=1, keepdims=True)
        cots[rows, :] = (scale * cots[rows, :].astype(F32)).astype(BF)

    for dx in (2, 1, 3, 0):
        base = ((x + dx) % 4) * (4 * ROWS)
        pick[...] = ones(iota((4 * ROWS, COPIES), 0) + base == row[...])

        @pl.loop(0, FF // UNIT)
        def _(part):
            cols = at(part * UNIT, UNIT)
            send[at(base, 4 * ROWS), cols] = jnp.dot(pick[...], cots[:, cols], preferred_element_type=F32).astype(BF)

    cot_sent = []

    def send_cots(low_row, high_row, got, index):
        size = high_row - low_row
        for part in range(size // 16):
            for peer in peers:
                copy = copy_to(
                    send.at[at(place(*peer) * ROWS + low_row + part * 16, 16)], got.at[at(me * size + part * 16, 16)],
                    cot_send.at[len(cot_sent)], cot_recv.at[index * NE + me], device(*peer),
                )
                copy.start()
                cot_sent.append(copy)
        got[at(me * size, size, 16), :] = send[at(me * ROWS + low_row, size, 16), :]

    def wait_cots(size, got, index):
        for peer in peers:
            ref = got.at[at(place(*peer) * size, size, 16)]
            copy_to(ref, ref, cot_send.at[0], cot_recv.at[index * NE + place(*peer)], device(*peer)).wait_recv()

    send_cots(0, EARLY, got_early, 0)

    arrive(1, 1, 0)
    to_right(1, 1, 0)
    to_left(1, 1, 0)
    to_sibling(1, 1, 0)
    arrive(0, 0, 3)
    to_right(0, 0, 3, 0)
    to_across(0, 3)
    to_sibling(0, 0, 3)
    arrive(0, 0, 1)
    to_left(0, 0, 1, 1)
    to_across(0, 1)
    to_sibling(0, 0, 1)

    index = iota((RJ, RJ), 0)
    turn = ones(iota((RJ, RJ), 1) == (index // RC * CH + index % CH) * R + (index % RC) // CH)
    loads[2].wait()
    loads[3].wait()

    @pl.loop(0, A_UNITS)
    def _(part):
        cols = at(part * UNIT, UNIT)
        a16[:, cols] = jnp.dot(turn, a[:, cols].astype(BF), preferred_element_type=F32).astype(BF)

    @pl.loop(0, B_UNITS)
    def _(part):
        cols = at(part * UNIT, UNIT)
        b16[:, cols] = jnp.dot(turn, b[:, cols].astype(BF), preferred_element_type=F32).astype(BF)

    arrive(0, 1, 0)
    to_sibling(0, 1, 0)
    arrive(1, 0, 3)
    to_right(1, 0, 3, 0)
    to_sibling(1, 0, 3)
    arrive(1, 0, 1)
    to_left(1, 0, 1, 1)
    to_sibling(1, 0, 1)

    for peer in peers:
        ref = ids_all.at[at(place(*peer) * TOP, TOP)]
        copy_to(ref, ref, ids_send.at[0], ids_recv.at[place(*peer)], device(*peer)).wait_recv()
    repeat = ones(iota((ROWS, J), 0) // CAP == iota((ROWS, J), 1))
    turn_in = (iota((ROWS, TOK), 0) % CAP).astype(F32)

    @pl.loop(0, NE)
    def _(source):
        ids = ids_all[at(source * TOP, TOP), :]
        hit = jnp.zeros((J, TOK), F32)
        for k in range(TOP):
            hit = hit + jnp.where(ids[k:k + 1, :] == iota((J, TOK), 0) + me * J, 1.0, 0.0)
        count = jnp.dot(hit.astype(BF), before, preferred_element_type=F32)
        value = jnp.where(hit > 0.5, count, -1.0)
        hot = ones(jnp.dot(repeat, value.astype(BF), preferred_element_type=F32) == turn_in)
        hot_early[at(source * EARLY, EARLY), :] = hot[:EARLY]
        hot_late[at(source * LATE, LATE), :] = hot[EARLY:]

    arrive(0, 0, 2, 0)
    arrive(0, 0, 2, 1)
    to_across(0, 2)
    to_sibling(0, 0, 2)
    arrive(1, 1, 3)
    to_right(1, 1, 3, 0)
    to_sibling(1, 1, 3)
    arrive(1, 1, 1)
    to_left(1, 1, 1, 1)
    to_sibling(1, 1, 1)
    send_cots(EARLY, ROWS, got_late, 1)
    arrive(0, 1, 3)
    to_sibling(0, 1, 3)
    arrive(0, 1, 1)
    to_sibling(0, 1, 1)
    arrive(1, 0, 2, 0)
    arrive(1, 0, 2, 1)
    to_sibling(1, 0, 2)
    arrive(1, 1, 2, 0)
    arrive(1, 1, 2, 1)
    to_sibling(1, 1, 2)
    arrive(0, 1, 2)
    to_sibling(0, 1, 2)
    for half in range(2):
        for dy in range(2):
            for dx in range(4):
                ref = block(dy, dx, 1, half, None)
                copy_to(ref, ref, tok_send.at[0], sib_slot(half, dy, dx), device(0, 0, 1)).wait_recv()

    @pl.loop(0, 4)
    def _(part):
        rows = at(part * UNIT, UNIT)
        low[rows, :] = contract(gathered[rows, :], a16[...], 1, 1).astype(BF)

    def own(size, base, chunk, count=1):
        line = iota((size * count, RC), 0) % size + base
        return line // CAP == iota((size * count, RC), 1) % CH + chunk * CH

    def backward(got, back, size, base, chunk):
        mask = own(size, base, chunk, 4)

        @pl.loop(0, 4)
        def _(part):
            rows = at(part * (4 * size), 4 * size)
            value = contract(got[rows, :], b16[chunk * RC:(chunk + 1) * RC, :], 1, 1)
            back[rows, :] = jnp.where(mask, value, 0.0).astype(BF)

    def hidden(hot, lows, size, base, chunk):
        mask = own(size, base, chunk)

        @pl.loop(0, NE)
        def _(source):
            rows = at(source * size, size)
            value = jnp.dot(
                hot[rows, :], low[at(source * TOK, TOK), chunk * RC:(chunk + 1) * RC], preferred_element_type=F32
            )
            lows[rows, :] = jnp.where(mask, value, 0.0).astype(BF)

    grad_sent = []

    def gradients(chunk):
        backward(got_early, back_early, EARLY, 0, chunk)
        hidden(hot_early, low_early, EARLY, 0, chunk)
        if chunk:
            backward(got_late, back_late, LATE, EARLY, chunk)
            hidden(hot_late, low_late, LATE, EARLY, chunk)

        @pl.loop(0, NE)
        def _(source):
            rows = at(source * EARLY, EARLY)
            value = contract(back_early[rows, :], hot_early[rows, :], 0, 0)
            if chunk:
                rows = at(source * LATE, LATE)
                value = value + contract(back_late[rows, :], hot_late[rows, :], 0, 0)
            weights[:, at(source * TOK, TOK)] = value.astype(BF)

        @pl.loop(0, D // 1024)
        def _(part):
            cols = at(part * 1024, 1024)
            grad_a[:, cols] = jnp.dot(weights[...], gathered[:, cols], preferred_element_type=F32)

        @pl.loop(0, B_UNITS)
        def _(part):
            cols = at(part * UNIT, UNIT)
            value = contract(low_early[...], got_early[:, cols], 0, 0)
            if chunk:
                value = value + contract(low_late[...], got_late[:, cols], 0, 0)
            grad_b[:, cols] = value

        def grad_unit(number):
            if number < A_UNITS * R:
                r, column = divmod(number, A_UNITS)
                return grad_a[r * CH:(r + 1) * CH, column * UNIT:(column + 1) * UNIT]
            r, column = divmod(number - A_UNITS * R, B_UNITS)
            return grad_b[r * CH:(r + 1) * CH, column * UNIT:(column + 1) * UNIT]

        for share in range(ND):
            for column in range(UNITS):
                parts = [grad_unit((share * 4 + quarter) * UNITS + column) for quarter in range(4)]
                wire[chunk, share * 16:(share + 1) * 16, column * UNIT:(column + 1) * UNIT] = jnp.concatenate(parts, axis=0).astype(BF)

        for step in (4, 1, 7, 3, 5, 2, 6):
            to = groups[step - 1]
            copy = copy_to(
                wire.at[chunk, at(to[0] * 16, 16)], wire_got.at[chunk, at(dp * 16, 16)],
                grad_send.at[chunk * ND + step], grad_recv.at[chunk * ND + dp], to,
            )
            copy.start()
            grad_sent.append(copy)
        wire_got[chunk, at(dp * 16, 16), :] = wire[chunk, at(dp * 16, 16), :]

    wait_cots(EARLY, got_early, 0)
    gradients(0)

    exact = lax.Precision.HIGHEST
    start = 4 * UNITS * dp
    a_first = jnp.minimum(start // A_UNITS, R - 8)
    b_first = jnp.clip((start - A_UNITS * R) // B_UNITS, 0, R - 16)

    def chooser(count, base):
        index = iota((count * J, RJ), 0)
        return (iota((count * J, RJ), 1) == (index % J) * R + index // J + base).astype(F32)

    @pl.loop(0, A_UNITS)
    def _(part):
        cols = at(part * UNIT, UNIT)
        rows_a[:, cols] = jnp.dot(chooser(8, a_first), a[:, cols], preferred_element_type=F32, precision=exact)

    @pl.loop(0, B_UNITS)
    def _(part):
        cols = at(part * UNIT, UNIT)
        rows_b[:, cols] = jnp.dot(chooser(16, b_first), b[:, cols], preferred_element_type=F32, precision=exact)

    @pl.loop(0, 4 * UNITS)
    def _(column):
        number = start + column
        in_a = jnp.clip(number // A_UNITS - a_first, 0, 7)
        number_b = jnp.maximum(number - A_UNITS * R, 0)
        in_b = jnp.clip(number_b // B_UNITS - b_first, 0, 15)
        value_a = rows_a[at(in_a * J, J), at(number % A_UNITS * UNIT, UNIT)]
        value_b = rows_b[at(in_b * J, J), at(number_b % B_UNITS * UNIT, UNIT)]
        param[:, at(column * UNIT, UNIT)] = jnp.where(number < A_UNITS * R, value_a, value_b)

    homes_now = homes_row[...].astype(F32).astype(BF)
    lane = iota((128, 128), 1)
    line = iota((128, 128), 0)
    dest = jnp.dot(homes_now, ones(line == me * J + lane % J), preferred_element_type=F32).astype(I32)
    named = ones(homes_row[...] == me * J + line % J)
    owner = contract(ones(iota((1, 128), 1) >= 0) * iota((1, 128), 1).astype(F32).astype(BF), named, 1, 1).astype(I32)
    stay = ones((line // J == lane // J) & (line % J == owner % J) & (owner // J == me))
    lane = iota((256, 128), 1)
    line = iota((256, 128), 0)
    same = (line % 16 == lane // J) & (line // 16 != me)
    leave = ones(same & (line // 16 == dest // J))
    enter = ones(same & (line // 16 == owner // J))

    wait_cots(LATE, got_late, 1)
    gradients(1)

    for chunk in range(2):
        for step in range(1, ND):
            source = (dp + step) % ND
            ref = wire_got.at[chunk, at(source * 16, 16)]
            copy_to(ref, ref, grad_send.at[0], grad_recv.at[chunk * ND + source], groups[step - 1]).wait_recv()
    loads[4].wait()
    loads[5].wait()

    fix_one = 1.0 - beta_one**adam_step
    fix_two = 1.0 - beta_two**adam_step
    for part in range(4):
        inside = pl.ds(part * PIECE, PIECE)
        totals = []
        for chunk in range(2):
            grad = wire_got[chunk, 0:16, inside].astype(F32)
            for source in range(1, ND):
                grad = grad + wire_got[chunk, source * 16:(source + 1) * 16, inside].astype(F32)
            totals.append(adapter_scale_factor * grad)
        for quarter in range(4):
            piece = quarter * 4 + part
            cols = pl.ds(piece * PIECE, PIECE)
            grad = jnp.concatenate([total[quarter * CH:(quarter + 1) * CH] for total in totals], axis=0)
            one = beta_one * first[:, cols] + (1.0 - beta_one) * grad
            two = beta_two * second[:, cols] + (1.0 - beta_two) * grad * grad
            old = param[:, cols]
            new = old - learn_rate * (one / fix_one / (jnp.sqrt(two / fix_two) + adam_eps) + decay_rate * old)
            for kind, value in enumerate((new, one, two)):
                moving[kind, piece * J:(piece + 1) * J, :] = value.astype(BF)

    move_sent = []

    def move(kind):
        packed[kind] = jnp.dot(leave, moving[kind], preferred_element_type=F32).astype(BF)
        landed[kind, at(me * 16, 16), :] = jnp.zeros((16, PIECE), BF)
        for step in (8, 9, 10, 11, 7, 6, 5, 4, 12, 13, 14, 15, 3, 2, 1):
            to = homes[step - 1]
            copy = copy_to(
                packed.at[kind, at(to[1] * 16, 16)], landed.at[kind, at(me * 16, 16)],
                move_send.at[kind * NE + step], move_recv.at[kind * NE + me], to,
            )
            copy.start()
            move_sent.append(copy)

    def arrived(kind):
        for step in range(1, NE):
            source = (me + step) % NE
            ref = landed.at[kind, at(source * 16, 16)]
            copy_to(ref, ref, move_send.at[0], move_recv.at[kind * NE + source], homes[step - 1]).wait_recv()
        return (contract(enter, landed[kind], 0, 0) + contract(stay, moving[kind], 0, 0)).astype(BF)

    move(0)
    whole[at(dp * 128, 128), :] = arrived(0)

    all_sent = []

    def group(dy, dz):
        return ((yl + dy) % 2) * 4 + (z + dz) % 4

    def part_of(dy, dz, late):
        size = 128 - Y_FIRST if late else Y_FIRST
        return whole.at[at(group(dy, dz) * 128 + (Y_FIRST if late else 0), size, 16)]

    def share_slot(dy, dz, late):
        return all_recv.at[(late * 2 + dy) * 4 + dz]

    def pass_on(dy, dz, late, to_y, to_z):
        ref = part_of(dy, dz, late)
        copy = copy_to(
            ref, ref, all_send.at[len(all_sent)], share_slot((dy + to_y) % 2, (dz - to_z) % 4, late), (group(to_y, to_z), me)
        )
        copy.start()
        all_sent.append(copy)

    def came(dy, dz, late):
        ref = part_of(dy, dz, late)
        copy_to(ref, ref, all_send.at[0], share_slot(dy, dz, late), groups[0]).wait_recv()

    pass_on(0, 0, 0, 1, 0)
    for step in (1, 3, 2):
        pass_on(0, 0, 1, 0, step)
    pass_on(0, 0, 1, 1, 0)
    for step in (1, 3, 2):
        pass_on(0, 0, 0, 0, step)
    move(1)
    move(2)
    came(1, 0, 0)
    for step in (1, 3, 2):
        pass_on(1, 0, 0, 0, step)
    for step in (1, 3, 2):
        came(0, step, 1)
        pass_on(0, step, 1, 1, 0)
    first_out[...] = arrived(1)
    second_out[...] = arrived(2)
    for step in (1, 3, 2):
        came(0, step, 0)
        came(1, step, 0)
    for step in range(4):
        came(1, step, 1)
    for copy in sent + small + cot_sent + grad_sent + move_sent + all_sent:
        copy.wait_send()


def finish_kernel(whole, first, second, new_a, new_b, new_first, new_second):
    index = iota((RJ, RJ), 0)
    turn = ones(iota((RJ, RJ), 1) == index % R * J + index // R)

    def unit(number):
        share, inside = divmod(number * UNIT, SHARE)
        parts = []
        left = UNIT
        while left:
            piece, offset = divmod(inside, PIECE)
            size = min(left, PIECE - offset)
            line = share * 128 + piece * J
            pair = whole[line // 16 * 16:line // 16 * 16 + 16, offset:offset + size].astype(F32)
            parts.append(pair[line % 16:line % 16 + J])
            left -= size
            inside += size
        return parts[0] if len(parts) == 1 else jnp.concatenate(parts, axis=1)

    for out, columns, base in ((new_a, A_UNITS, 0), (new_b, B_UNITS, A_UNITS * R)):
        for column in range(columns):
            stack = jnp.concatenate([unit(base + r * columns + column) for r in range(R)], axis=0).astype(BF)
            out[:, column * UNIT:(column + 1) * UNIT] = jnp.dot(turn, stack, preferred_element_type=F32)
    for out, value in ((new_first, first), (new_second, second)):
        for pair in range(8):
            both = value[pair * 16:(pair + 1) * 16, :].astype(F32)
            out[:, 2 * pair * PIECE:(2 * pair + 1) * PIECE] = both[:J]
            out[:, (2 * pair + 1) * PIECE:(2 * pair + 2) * PIECE] = both[J:]


def vmem(count):
    return [pl.BlockSpec(memory_space=pltpu.VMEM)] * count


def anywhere(count):
    return [pl.BlockSpec(memory_space=pl.ANY)] * count


def shards(tokens, up_grad, gate_weights, expert_ids, new_home, adapter_a, adapter_b, first_moment, second_moment):
    dma = pltpu.SemaphoreType.DMA
    whole, first, second = pl.pallas_call(
        main_kernel,
        out_shape=[
            jax.ShapeDtypeStruct((ND * 128, PIECE), BF),
            jax.ShapeDtypeStruct((128, PIECE), BF),
            jax.ShapeDtypeStruct((128, PIECE), BF),
        ],
        in_specs=anywhere(2) + vmem(3) + anywhere(4),
        out_specs=vmem(3),
        scratch_shapes=[
            pltpu.VMEM((NE * TOK, D), BF),
            pltpu.VMEM((COPIES, FF), BF),
            pltpu.VMEM((NE * ROWS, FF), BF),
            pltpu.VMEM((NE * EARLY, FF), BF),
            pltpu.VMEM((NE * LATE, FF), BF),
            pltpu.VMEM((NE * TOP, TOK), I32),
            pltpu.VMEM((RJ, D), F32),
            pltpu.VMEM((RJ, FF), F32),
            pltpu.VMEM((RJ, D), BF),
            pltpu.VMEM((RJ, FF), BF),
            pltpu.VMEM((4 * ROWS, COPIES), BF),
            pltpu.VMEM((NE * EARLY, TOK), BF),
            pltpu.VMEM((NE * LATE, TOK), BF),
            pltpu.VMEM((NE * TOK, RJ), BF),
            pltpu.VMEM((RC, NE * TOK), BF),
            pltpu.VMEM((NE * EARLY, RC), BF),
            pltpu.VMEM((NE * LATE, RC), BF),
            pltpu.VMEM((NE * EARLY, RC), BF),
            pltpu.VMEM((NE * LATE, RC), BF),
            pltpu.VMEM((RC, D), F32),
            pltpu.VMEM((RC, FF), F32),
            pltpu.VMEM((1, COPIES), I32),
            pltpu.VMEM((2, ND * 16, QUARTER), BF),
            pltpu.VMEM((2, ND * 16, QUARTER), BF),
            pltpu.VMEM((J, SHARE), F32),
            pltpu.VMEM((J, SHARE), F32),
            pltpu.VMEM((8 * J, D), F32),
            pltpu.VMEM((16 * J, FF), F32),
            pltpu.VMEM((J, SHARE), F32),
            pltpu.VMEM((3, 128, PIECE), BF),
            pltpu.VMEM((3, 256, PIECE), BF),
            pltpu.VMEM((3, 256, PIECE), BF),
            dma((6,)),
            dma((NE,)),
            dma((NE,)),
            dma((NE * 5,)),
            dma((2 * NE,)),
            dma((64,)),
            dma((32,)),
            dma((16,)),
            dma((2 * ND,)),
            dma((2 * ND,)),
            dma((3 * NE,)),
            dma((3 * NE,)),
            dma((16,)),
            dma((16,)),
        ],
        compiler_params=pltpu.CompilerParams(collective_id=0, has_side_effects=True, vmem_limit_bytes=63 * 2**20),
        name="dispatch_update",
    )(
        tokens, up_grad.reshape(COPIES, FF), gate_weights.T, expert_ids.T, new_home.reshape(1, NE * J),
        adapter_a.reshape(RJ, D), adapter_b.reshape(RJ, FF), first_moment, second_moment,
    )
    new_a, new_b, new_first, new_second = pl.pallas_call(
        finish_kernel,
        out_shape=[
            jax.ShapeDtypeStruct((RJ, D), F32),
            jax.ShapeDtypeStruct((RJ, FF), F32),
            jax.ShapeDtypeStruct((J, SHARE), F32),
            jax.ShapeDtypeStruct((J, SHARE), F32),
        ],
        in_specs=vmem(3),
        out_specs=vmem(4),
        compiler_params=pltpu.CompilerParams(vmem_limit_bytes=60 * 2**20),
        name="finish",
    )(whole, first, second)
    return new_a.reshape(J, R, D), new_b.reshape(J, R, FF), new_first, new_second


def solution(mesh):
    placed = (
        P(("dp", "expert"), None),
        P(("dp", "expert"), None, None),
        P(("dp", "expert"), None),
        P(("dp", "expert"), None),
        P(),
        P("expert", None, None),
        P("expert", None, None),
        P("expert", "dp"),
        P("expert", "dp"),
    )
    return jax.shard_map(
        shards,
        mesh=mesh,
        in_specs=placed,
        out_specs=(P("expert", None, None), P("expert", None, None), P("expert", "dp"), P("expert", "dp")),
        check_vma=False,
    )
```

time: 259 us -> 215 us (0.83)
  Pallas kernels: 252 us -> 213 us
  local copies, waits for them, and re-layouts: 3.97 us -> 0 us
    pallas_call x2 -> x1, Pallas kernels: 246 us -> 208 us  [shards(): pl.pallas_call(main_kernel, out_shape=[jax.ShapeDtypeStruct((ND * 128, PI...]
where the time goes in v2:
time: 215 us; the launch traced here: 214 us
  Pallas kernels  213 us (99%)
    pallas_call x1, Pallas kernels, shards(): pl.pallas_call(main_kernel, out_shape=[jax.ShapeDtypeStruct((ND * 128, PI...  208 us
    pallas_call x1, Pallas kernels, shards(): pl.pallas_call(finish_kernel, out_shape=[jax.ShapeDtypeStruct((RJ, D), F3...  5.61 us

profile of v2, /device:TPU:1, one launch (start us, length us, event | category | flops | bytes accessed | tf_op | source)
XLA Modules:
  0.0 213.9 jit_solution(6694993865987310574)
XLA Ops:
  0.6 207.7 %dispatch_update.1 = (bf16[1024,1408]{1,0:T(8,128)(2,1)}, bf16[128,1408]{1,0:T(8,128)(2,1)}, bf16[128,1408]{1,0:T(8,128)(2,1)}) custom-call(bf16[128,4096]{1,0:T(8,128)(2,1)} %tok.1, bf16[1024,1536]{1,0:T(8,128)(2,1)} %bitcast.9, f32[8,128]{1,0:T(8,128)} %bitcast.11, s32[8,128]{1,0:T(8,128)} %bitcast.12, s32[1,128]{1,0:T(1,128)} %bitcast.13, ...), custom_call_target="tpu_custom_call" | custom-call | tf_op jit(solution)/shard_map/dispatch_update/pallas_call | solution.py:581
  208.3 5.6 %finish.1 = (f32[256,4096]{1,0:T(8,128)}, f32[256,1536]{1,0:T(8,128)}, f32[8,22528]{1,0:T(8,128)}, f32[8,22528]{1,0:T(8,128)}) custom-call(bf16[1024,1408]{1,0:T(8,128)(2,1)} %get-tuple-element.11.whole, bf16[128,1408]{1,0:T(8,128)(2,1)} %get-tuple-element.12.first, bf16[128,1408]{1,0:T(8,128)(2,1)} %get-tuple-element.13.second), custom_call_target="tpu_custom_call" | custom-call | tf_op jit(solution)/shard_map/finish/pallas_call | solution.py:644

commit v3 on v2

--- a/solution.py
+++ b/solution.py
@@ -36,8 +36,8 @@
 UNITS = QUARTER // UNIT
 A_UNITS = D // UNIT
 B_UNITS = FF // UNIT
-SPLIT = 1536
-Y_FIRST = 48
+SPLIT = 1792
+SUBS = ((0, 768), (768, 640))
 
 MESH = pl.DeviceIdType.MESH
 BF = jnp.bfloat16
@@ -266,7 +266,7 @@
     repeat = ones(iota((ROWS, J), 0) // CAP == iota((ROWS, J), 1))
     turn_in = (iota((ROWS, TOK), 0) % CAP).astype(F32)
 
-    @pl.loop(0, NE)
+    @pl.loop(0, NE, unroll=4)
     def _(source):
         ids = ids_all[at(source * TOP, TOP), :]
         hit = jnp.zeros((J, TOK), F32)
@@ -278,6 +278,29 @@
         hot_early[at(source * EARLY, EARLY), :] = hot[:EARLY]
         hot_late[at(source * LATE, LATE), :] = hot[EARLY:]
 
+    def own(size, base, columns, first_column):
+        line = iota((size, columns), 0) + base
+        column = iota((size, columns), 1) + first_column
+        return line // CAP == column // RC * CH + column % CH
+
+    def from_sibling(dx):
+        for half in range(2):
+            for dy in range(2):
+                ref = block(dy, dx, 1, half, None)
+                copy_to(ref, ref, tok_send.at[0], sib_slot(half, dy, dx), device(0, 0, 1)).wait_recv()
+
+    def hidden(dx):
+        from_sibling(dx)
+        base = (x + dx) % 4
+        rows = at(base * 4 * TOK, 4 * TOK)
+        low[...] = contract(gathered[rows, :], a16[...], 1, 1).astype(BF)
+        for hots, lows, size, first_row in ((hot_early, low_early, EARLY, 0), (hot_late, low_late, LATE, EARLY)):
+            mask = own(size, first_row, RJ, 0)
+            for inside in range(4):
+                rows = at((base * 4 + inside) * size, size, 16)
+                value = jnp.dot(hots[rows, :], low[inside * TOK:(inside + 1) * TOK, :], preferred_element_type=F32)
+                lows[rows, :] = jnp.where(mask, value, 0.0).astype(BF)
+
     arrive(0, 0, 2, 0)
     arrive(0, 0, 2, 1)
     to_across(0, 2)
@@ -288,7 +311,7 @@
     arrive(1, 1, 1)
     to_left(1, 1, 1, 1)
     to_sibling(1, 1, 1)
-    send_cots(EARLY, ROWS, got_late, 1)
+    hidden(0)
     arrive(0, 1, 3)
     to_sibling(0, 1, 3)
     arrive(0, 1, 1)
@@ -296,62 +319,75 @@
     arrive(1, 0, 2, 0)
     arrive(1, 0, 2, 1)
     to_sibling(1, 0, 2)
+    send_cots(EARLY, ROWS, got_late, 1)
+    hidden(3)
+    hidden(1)
     arrive(1, 1, 2, 0)
     arrive(1, 1, 2, 1)
     to_sibling(1, 1, 2)
     arrive(0, 1, 2)
     to_sibling(0, 1, 2)
-    for half in range(2):
-        for dy in range(2):
-            for dx in range(4):
-                ref = block(dy, dx, 1, half, None)
-                copy_to(ref, ref, tok_send.at[0], sib_slot(half, dy, dx), device(0, 0, 1)).wait_recv()
-
-    @pl.loop(0, 4)
-    def _(part):
-        rows = at(part * UNIT, UNIT)
-        low[rows, :] = contract(gathered[rows, :], a16[...], 1, 1).astype(BF)
-
-    def own(size, base, chunk, count=1):
-        line = iota((size * count, RC), 0) % size + base
-        return line // CAP == iota((size * count, RC), 1) % CH + chunk * CH
-
-    def backward(got, back, size, base, chunk):
-        mask = own(size, base, chunk, 4)
+    hidden(2)
+
+    def backward(got, back, size, base, first_column):
+        columns = RJ - first_column
+        mask = jnp.concatenate([own(size, base, columns, first_column)] * 4, axis=0)
 
         @pl.loop(0, 4)
         def _(part):
             rows = at(part * (4 * size), 4 * size)
-            value = contract(got[rows, :], b16[chunk * RC:(chunk + 1) * RC, :], 1, 1)
-            back[rows, :] = jnp.where(mask, value, 0.0).astype(BF)
-
-    def hidden(hot, lows, size, base, chunk):
-        mask = own(size, base, chunk)
-
-        @pl.loop(0, NE)
-        def _(source):
-            rows = at(source * size, size)
-            value = jnp.dot(
-                hot[rows, :], low[at(source * TOK, TOK), chunk * RC:(chunk + 1) * RC], preferred_element_type=F32
+            value = contract(got[rows, :], b16[first_column:, :], 1, 1)
+            back[rows, first_column:] = jnp.where(mask, value, 0.0).astype(BF)
+
+    def grad_flat(number, size):
+        parts = []
+        while size:
+            if number < R * D:
+                ref, (r, column), width = grad_a, divmod(number, D), D
+            else:
+                ref, (r, column), width = grad_b, divmod(number - R * D, FF), FF
+            step = min(size, width - column)
+            parts.append(ref[r * CH:(r + 1) * CH, column:column + step])
+            number += step
+            size -= step
+        return parts[0] if len(parts) == 1 else jnp.concatenate(parts, axis=1)
+
+    grad_sent = []
+
+    def send_grads(chunk, cols, index):
+        for step in (4, 1, 7, 3, 5, 2, 6):
+            to = groups[step - 1]
+            copy = copy_to(
+                wire.at[chunk, at(to[0] * 16, 16), cols], wire_got.at[chunk, at(dp * 16, 16), cols],
+                grad_send.at[index * ND + step], grad_recv.at[index * ND + dp], to,
             )
-            lows[rows, :] = jnp.where(mask, value, 0.0).astype(BF)
-
-    grad_sent = []
+            copy.start()
+            grad_sent.append(copy)
+        wire_got[chunk, at(dp * 16, 16), cols] = wire[chunk, at(dp * 16, 16), cols]
+
+    def wait_grads(chunk, cols, index):
+        for step in range(1, ND):
+            source = (dp + step) % ND
+            ref = wire_got.at[chunk, at(source * 16, 16), cols]
+            copy_to(ref, ref, grad_send.at[0], grad_recv.at[index * ND + source], groups[step - 1]).wait_recv()
+
+    def wire_cols(sub):
+        return pl.ds(4 * SUBS[sub][0], 4 * SUBS[sub][1])
 
     def gradients(chunk):
-        backward(got_early, back_early, EARLY, 0, chunk)
-        hidden(hot_early, low_early, EARLY, 0, chunk)
+        chunk_cols = slice(chunk * RC, (chunk + 1) * RC)
         if chunk:
-            backward(got_late, back_late, LATE, EARLY, chunk)
-            hidden(hot_late, low_late, LATE, EARLY, chunk)
-
-        @pl.loop(0, NE)
+            backward(got_late, back_late, LATE, EARLY, RC)
+        else:
+            backward(got_early, back_early, EARLY, 0, 0)
+
+        @pl.loop(0, NE, unroll=8)
         def _(source):
             rows = at(source * EARLY, EARLY)
-            value = contract(back_early[rows, :], hot_early[rows, :], 0, 0)
+            value = contract(back_early[rows, chunk_cols], hot_early[rows, :], 0, 0)
             if chunk:
                 rows = at(source * LATE, LATE)
-                value = value + contract(back_late[rows, :], hot_late[rows, :], 0, 0)
+                value = value + contract(back_late[rows, chunk_cols], hot_late[rows, :], 0, 0)
             weights[:, at(source * TOK, TOK)] = value.astype(BF)
 
         @pl.loop(0, D // 1024)
@@ -362,32 +398,22 @@
         @pl.loop(0, B_UNITS)
         def _(part):
             cols = at(part * UNIT, UNIT)
-            value = contract(low_early[...], got_early[:, cols], 0, 0)
+            value = contract(low_early[:, chunk_cols], got_early[:, cols], 0, 0)
             if chunk:
-                value = value + contract(low_late[...], got_late[:, cols], 0, 0)
+                value = value + contract(low_late[:, chunk_cols], got_late[:, cols], 0, 0)
             grad_b[:, cols] = value
 
-        def grad_unit(number):
-            if number < A_UNITS * R:
-                r, column = divmod(number, A_UNITS)
-                return grad_a[r * CH:(r + 1) * CH, column * UNIT:(column + 1) * UNIT]
-            r, column = divmod(number - A_UNITS * R, B_UNITS)
-            return grad_b[r * CH:(r + 1) * CH, column * UNIT:(column + 1) * UNIT]
-
-        for share in range(ND):
-            for column in range(UNITS):
-                parts = [grad_unit((share * 4 + quarter) * UNITS + column) for quarter in range(4)]
-                wire[chunk, share * 16:(share + 1) * 16, column * UNIT:(column + 1) * UNIT] = jnp.concatenate(parts, axis=0).astype(BF)
-
-        for step in (4, 1, 7, 3, 5, 2, 6):
-            to = groups[step - 1]
-            copy = copy_to(
-                wire.at[chunk, at(to[0] * 16, 16)], wire_got.at[chunk, at(dp * 16, 16)],
-                grad_send.at[chunk * ND + step], grad_recv.at[chunk * ND + dp], to,
-            )
-            copy.start()
-            grad_sent.append(copy)
-        wire_got[chunk, at(dp * 16, 16), :] = wire[chunk, at(dp * 16, 16), :]
+        for sub, (offset, size) in enumerate(SUBS):
+            for share in range(ND):
+                for part in range(4):
+                    base = share * SHARE + part * PIECE + offset
+                    value = jnp.concatenate([grad_flat(base + quarter * QUARTER, size) for quarter in range(4)], axis=0)
+                    col = 4 * offset + part * size
+                    wire[chunk, share * 16:(share + 1) * 16, col:col + size] = value.astype(BF)
+            if chunk:
+                send_grads(1, wire_cols(sub), 1 + sub)
+        if not chunk:
+            send_grads(0, pl.ds(0, QUARTER), 0)
 
     wait_cots(EARLY, got_early, 0)
     gradients(0)
@@ -437,104 +463,110 @@
     wait_cots(LATE, got_late, 1)
     gradients(1)
 
-    for chunk in range(2):
-        for step in range(1, ND):
-            source = (dp + step) % ND
-            ref = wire_got.at[chunk, at(source * 16, 16)]
-            copy_to(ref, ref, grad_send.at[0], grad_recv.at[chunk * ND + source], groups[step - 1]).wait_recv()
     loads[4].wait()
     loads[5].wait()
-
     fix_one = 1.0 - beta_one**adam_step
     fix_two = 1.0 - beta_two**adam_step
-    for part in range(4):
-        inside = pl.ds(part * PIECE, PIECE)
-        totals = []
-        for chunk in range(2):
-            grad = wire_got[chunk, 0:16, inside].astype(F32)
-            for source in range(1, ND):
-                grad = grad + wire_got[chunk, source * 16:(source + 1) * 16, inside].astype(F32)
-            totals.append(adapter_scale_factor * grad)
-        for quarter in range(4):
-            piece = quarter * 4 + part
-            cols = pl.ds(piece * PIECE, PIECE)
-            grad = jnp.concatenate([total[quarter * CH:(quarter + 1) * CH] for total in totals], axis=0)
-            one = beta_one * first[:, cols] + (1.0 - beta_one) * grad
-            two = beta_two * second[:, cols] + (1.0 - beta_two) * grad * grad
-            old = param[:, cols]
-            new = old - learn_rate * (one / fix_one / (jnp.sqrt(two / fix_two) + adam_eps) + decay_rate * old)
-            for kind, value in enumerate((new, one, two)):
-                moving[kind, piece * J:(piece + 1) * J, :] = value.astype(BF)
+
+    def update(sub):
+        offset, size = SUBS[sub]
+        for part in range(4):
+            inside = pl.ds(4 * offset + part * size, size)
+            totals = []
+            for chunk in range(2):
+                grad = wire_got[chunk, 0:16, inside].astype(F32)
+                for source in range(1, ND):
+                    grad = grad + wire_got[chunk, source * 16:(source + 1) * 16, inside].astype(F32)
+                totals.append(adapter_scale_factor * grad)
+            for quarter in range(4):
+                piece = quarter * 4 + part
+                cols = pl.ds(piece * PIECE + offset, size)
+                grad = jnp.concatenate([total[quarter * CH:(quarter + 1) * CH] for total in totals], axis=0)
+                one = beta_one * first[:, cols] + (1.0 - beta_one) * grad
+                two = beta_two * second[:, cols] + (1.0 - beta_two) * grad * grad
+                old = param[:, cols]
+                new = old - learn_rate * (one / fix_one / (jnp.sqrt(two / fix_two) + adam_eps) + decay_rate * old)
+                for kind, value in enumerate((new, one, two)):
+                    moving[kind, piece * J:(piece + 1) * J, pl.ds(offset, size)] = value.astype(BF)
 
     move_sent = []
 
-    def move(kind):
-        packed[kind] = jnp.dot(leave, moving[kind], preferred_element_type=F32).astype(BF)
-        landed[kind, at(me * 16, 16), :] = jnp.zeros((16, PIECE), BF)
+    def move(kind, cols, index):
+        packed[kind, :, cols] = jnp.dot(leave, moving[kind, :, cols], preferred_element_type=F32).astype(BF)
+        landed[kind, at(me * 16, 16), cols] = jnp.zeros((16, cols.size), BF)
         for step in (8, 9, 10, 11, 7, 6, 5, 4, 12, 13, 14, 15, 3, 2, 1):
             to = homes[step - 1]
             copy = copy_to(
-                packed.at[kind, at(to[1] * 16, 16)], landed.at[kind, at(me * 16, 16)],
-                move_send.at[kind * NE + step], move_recv.at[kind * NE + me], to,
+                packed.at[kind, at(to[1] * 16, 16), cols], landed.at[kind, at(me * 16, 16), cols],
+                move_send.at[index * NE + step], move_recv.at[index * NE + me], to,
             )
             copy.start()
             move_sent.append(copy)
 
-    def arrived(kind):
+    def arrived(kind, cols, index):
         for step in range(1, NE):
             source = (me + step) % NE
-            ref = landed.at[kind, at(source * 16, 16)]
-            copy_to(ref, ref, move_send.at[0], move_recv.at[kind * NE + source], homes[step - 1]).wait_recv()
-        return (contract(enter, landed[kind], 0, 0) + contract(stay, moving[kind], 0, 0)).astype(BF)
-
-    move(0)
-    whole[at(dp * 128, 128), :] = arrived(0)
+            ref = landed.at[kind, at(source * 16, 16), cols]
+            copy_to(ref, ref, move_send.at[0], move_recv.at[index * NE + source], homes[step - 1]).wait_recv()
+        return (contract(enter, landed[kind, :, cols], 0, 0) + contract(stay, moving[kind, :, cols], 0, 0)).astype(BF)
 
     all_sent = []
 
     def group(dy, dz):
         return ((yl + dy) % 2) * 4 + (z + dz) % 4
 
-    def part_of(dy, dz, late):
-        size = 128 - Y_FIRST if late else Y_FIRST
-        return whole.at[at(group(dy, dz) * 128 + (Y_FIRST if late else 0), size, 16)]
-
-    def share_slot(dy, dz, late):
-        return all_recv.at[(late * 2 + dy) * 4 + dz]
-
-    def pass_on(dy, dz, late, to_y, to_z):
-        ref = part_of(dy, dz, late)
+    def part_of(dy, dz, sub, half):
+        rows = at(group(dy, dz) * 128, 128) if half is None else at(group(dy, dz) * 128 + half * 64, 64)
+        return whole.at[rows, pl.ds(*SUBS[sub])]
+
+    def share_slot(dy, dz, sub, half):
+        return all_recv.at[((sub * 2 + dy) * 4 + dz) * 2 + (half or 0)]
+
+    def pass_on(dy, dz, sub, to_y, to_z, half=None):
+        ref = part_of(dy, dz, sub, half)
         copy = copy_to(
-            ref, ref, all_send.at[len(all_sent)], share_slot((dy + to_y) % 2, (dz - to_z) % 4, late), (group(to_y, to_z), me)
+            ref, ref, all_send.at[len(all_sent)], share_slot((dy + to_y) % 2, (dz - to_z) % 4, sub, half), (group(to_y, to_z), me)
         )
         copy.start()
         all_sent.append(copy)
 
-    def came(dy, dz, late):
-        ref = part_of(dy, dz, late)
-        copy_to(ref, ref, all_send.at[0], share_slot(dy, dz, late), groups[0]).wait_recv()
-
-    pass_on(0, 0, 0, 1, 0)
-    for step in (1, 3, 2):
-        pass_on(0, 0, 1, 0, step)
-    pass_on(0, 0, 1, 1, 0)
-    for step in (1, 3, 2):
-        pass_on(0, 0, 0, 0, step)
-    move(1)
-    move(2)
-    came(1, 0, 0)
-    for step in (1, 3, 2):
-        pass_on(1, 0, 0, 0, step)
-    for step in (1, 3, 2):
-        came(0, step, 1)
-        pass_on(0, step, 1, 1, 0)
-    first_out[...] = arrived(1)
-    second_out[...] = arrived(2)
-    for step in (1, 3, 2):
-        came(0, step, 0)
-        came(1, step, 0)
-    for step in range(4):
-        came(1, step, 1)
+    def came(dy, dz, sub, half=None):
+        ref = part_of(dy, dz, sub, half)
+        copy_to(ref, ref, all_send.at[0], share_slot(dy, dz, sub, half), groups[0]).wait_recv()
+
+    wait_grads(0, pl.ds(0, QUARTER), 0)
+    for sub in range(2):
+        wait_grads(1, wire_cols(sub), 1 + sub)
+        update(sub)
+        move(0, pl.ds(*SUBS[sub]), sub)
+    for sub in range(2):
+        cols = pl.ds(*SUBS[sub])
+        whole[at(dp * 128, 128), cols] = arrived(0, cols, sub)
+        pass_on(0, 0, sub, 1, 0)
+        pass_on(0, 0, sub, 0, 1)
+        pass_on(0, 0, sub, 0, 3)
+    full = pl.ds(0, PIECE)
+    move(1, full, 2)
+    move(2, full, 3)
+    for sub in range(2):
+        came(1, 0, sub)
+        pass_on(1, 0, sub, 0, 1)
+        pass_on(1, 0, sub, 0, 3)
+        came(0, 3, sub)
+        pass_on(0, 3, sub, 0, 1, 0)
+        came(0, 1, sub)
+        pass_on(0, 1, sub, 0, 3, 1)
+    for sub in range(2):
+        came(1, 3, sub)
+        pass_on(1, 3, sub, 0, 1, 0)
+        came(1, 1, sub)
+        pass_on(1, 1, sub, 0, 3, 1)
+    first_out[...] = arrived(1, full, 2)
+    second_out[...] = arrived(2, full, 3)
+    for sub in range(2):
+        for half in range(2):
+            came(0, 2, sub, half)
+            came(1, 2, sub, half)
     for copy in sent + small + cot_sent + grad_sent + move_sent + all_sent:
         copy.wait_send()
 
@@ -601,12 +633,12 @@
             pltpu.VMEM((4 * ROWS, COPIES), BF),
             pltpu.VMEM((NE * EARLY, TOK), BF),
             pltpu.VMEM((NE * LATE, TOK), BF),
-            pltpu.VMEM((NE * TOK, RJ), BF),
+            pltpu.VMEM((4 * TOK, RJ), BF),
             pltpu.VMEM((RC, NE * TOK), BF),
-            pltpu.VMEM((NE * EARLY, RC), BF),
-            pltpu.VMEM((NE * LATE, RC), BF),
-            pltpu.VMEM((NE * EARLY, RC), BF),
-            pltpu.VMEM((NE * LATE, RC), BF),
+            pltpu.VMEM((NE * EARLY, RJ), BF),
+            pltpu.VMEM((NE * LATE, RJ), BF),
+            pltpu.VMEM((NE * EARLY, RJ), BF),
+            pltpu.VMEM((NE * LATE, RJ), BF),
             pltpu.VMEM((RC, D), F32),
             pltpu.VMEM((RC, FF), F32),
             pltpu.VMEM((1, COPIES), I32),
@@ -628,12 +660,12 @@
             dma((64,)),
             dma((32,)),
             dma((16,)),
-            dma((2 * ND,)),
-            dma((2 * ND,)),
-            dma((3 * NE,)),
-            dma((3 * NE,)),
-            dma((16,)),
-            dma((16,)),
+            dma((3 * ND,)),
+            dma((3 * ND,)),
+            dma((4 * NE,)),
+            dma((4 * NE,)),
+            dma((32,)),
+            dma((32,)),
         ],
         compiler_params=pltpu.CompilerParams(collective_id=0, has_side_effects=True, vmem_limit_bytes=63 * 2**20),
         name="dispatch_update",

time: 215 us -> 190 us (0.88)
  the two profiles are of different devices: /device:TPU:1 before, /device:TPU:28 now
where the time goes in v3:
time: 190 us
  Pallas kernels  189 us (99%)
    pallas_call x1, Pallas kernels, shards(): pl.pallas_call(main_kernel, out_shape=[jax.ShapeDtypeStruct((ND * 128, PI...  183 us
    pallas_call x1, Pallas kernels, shards(): pl.pallas_call(finish_kernel, out_shape=[jax.ShapeDtypeStruct((RJ, D), F3...  5.61 us

profile of v3, /device:TPU:28, one launch (start us, length us, event | category | flops | bytes accessed | tf_op | source)
XLA Modules:
  0.0 189.7 jit_solution(3344320576418520157)
XLA Ops:
  0.6 183.4 %dispatch_update.1 = (bf16[1024,1408]{1,0:T(8,128)(2,1)}, bf16[128,1408]{1,0:T(8,128)(2,1)}, bf16[128,1408]{1,0:T(8,128)(2,1)}) custom-call(bf16[128,4096]{1,0:T(8,128)(2,1)} %tok.1, bf16[1024,1536]{1,0:T(8,128)(2,1)} %bitcast.9, f32[8,128]{1,0:T(8,128)} %bitcast.11, s32[8,128]{1,0:T(8,128)} %bitcast.12, s32[1,128]{1,0:T(1,128)} %bitcast.13, ...), custom_call_target="tpu_custom_call" | custom-call | tf_op jit(solution)/shard_map/dispatch_update/pallas_call | solution.py:613
  184.1 5.6 %finish.1 = (f32[256,4096]{1,0:T(8,128)}, f32[256,1536]{1,0:T(8,128)}, f32[8,22528]{1,0:T(8,128)}, f32[8,22528]{1,0:T(8,128)}) custom-call(bf16[1024,1408]{1,0:T(8,128)(2,1)} %get-tuple-element.11.whole, bf16[128,1408]{1,0:T(8,128)(2,1)} %get-tuple-element.12.first, bf16[128,1408]{1,0:T(8,128)(2,1)} %get-tuple-element.13.second), custom_call_target="tpu_custom_call" | custom-call | tf_op jit(solution)/shard_map/finish/pallas_call | solution.py:676

commit v4 on v3

--- a/solution.py
+++ b/solution.py
@@ -221,8 +221,6 @@
             ref = got.at[at(place(*peer) * size, size, 16)]
             copy_to(ref, ref, cot_send.at[0], cot_recv.at[index * NE + place(*peer)], device(*peer)).wait_recv()
 
-    send_cots(0, EARLY, got_early, 0)
-
     arrive(1, 1, 0)
     to_right(1, 1, 0)
     to_left(1, 1, 0)
@@ -235,6 +233,7 @@
     to_left(0, 0, 1, 1)
     to_across(0, 1)
     to_sibling(0, 0, 1)
+    send_cots(0, EARLY, got_early, 0)
 
     index = iota((RJ, RJ), 0)
     turn = ones(iota((RJ, RJ), 1) == (index // RC * CH + index % CH) * R + (index % RC) // CH)
@@ -259,6 +258,40 @@
     arrive(1, 0, 1)
     to_left(1, 0, 1, 1)
     to_sibling(1, 0, 1)
+
+    def own(size, base, columns, first_column):
+        line = iota((size, columns), 0) + base
+        column = iota((size, columns), 1) + first_column
+        return line // CAP == column // RC * CH + column % CH
+
+    def from_sibling(dx):
+        for half in range(2):
+            for dy in range(2):
+                ref = block(dy, dx, 1, half, None)
+                copy_to(ref, ref, tok_send.at[0], sib_slot(half, dy, dx), device(0, 0, 1)).wait_recv()
+
+    def hidden(dx):
+        from_sibling(dx)
+        base = (x + dx) % 4
+        rows = at(base * 4 * TOK, 4 * TOK)
+        low[...] = contract(gathered[rows, :], a16[...], 1, 1).astype(BF)
+        for hots, lows, size, first_row in ((hot_early, low_early, EARLY, 0), (hot_late, low_late, LATE, EARLY)):
+            mask = own(size, first_row, RJ, 0)
+            for inside in range(4):
+                rows = at((base * 4 + inside) * size, size, 16)
+                value = jnp.dot(hots[rows, :], low[inside * TOK:(inside + 1) * TOK, :], preferred_element_type=F32)
+                lows[rows, :] = jnp.where(mask, value, 0.0).astype(BF)
+
+    arrive(0, 0, 2, 0)
+    arrive(0, 0, 2, 1)
+    to_across(0, 2)
+    to_sibling(0, 0, 2)
+    arrive(1, 1, 3)
+    to_right(1, 1, 3, 0)
+    to_sibling(1, 1, 3)
+    arrive(1, 1, 1)
+    to_left(1, 1, 1, 1)
+    to_sibling(1, 1, 1)
 
     for peer in peers:
         ref = ids_all.at[at(place(*peer) * TOP, TOP)]
@@ -278,39 +311,6 @@
         hot_early[at(source * EARLY, EARLY), :] = hot[:EARLY]
         hot_late[at(source * LATE, LATE), :] = hot[EARLY:]
 
-    def own(size, base, columns, first_column):
-        line = iota((size, columns), 0) + base
-        column = iota((size, columns), 1) + first_column
-        return line // CAP == column // RC * CH + column % CH
-
-    def from_sibling(dx):
-        for half in range(2):
-            for dy in range(2):
-                ref = block(dy, dx, 1, half, None)
-                copy_to(ref, ref, tok_send.at[0], sib_slot(half, dy, dx), device(0, 0, 1)).wait_recv()
-
-    def hidden(dx):
-        from_sibling(dx)
-        base = (x + dx) % 4
-        rows = at(base * 4 * TOK, 4 * TOK)
-        low[...] = contract(gathered[rows, :], a16[...], 1, 1).astype(BF)
-        for hots, lows, size, first_row in ((hot_early, low_early, EARLY, 0), (hot_late, low_late, LATE, EARLY)):
-            mask = own(size, first_row, RJ, 0)
-            for inside in range(4):
-                rows = at((base * 4 + inside) * size, size, 16)
-                value = jnp.dot(hots[rows, :], low[inside * TOK:(inside + 1) * TOK, :], preferred_element_type=F32)
-                lows[rows, :] = jnp.where(mask, value, 0.0).astype(BF)
-
-    arrive(0, 0, 2, 0)
-    arrive(0, 0, 2, 1)
-    to_across(0, 2)
-    to_sibling(0, 0, 2)
-    arrive(1, 1, 3)
-    to_right(1, 1, 3, 0)
-    to_sibling(1, 1, 3)
-    arrive(1, 1, 1)
-    to_left(1, 1, 1, 1)
-    to_sibling(1, 1, 1)
     hidden(0)
     arrive(0, 1, 3)
     to_sibling(0, 1, 3)
@@ -327,7 +327,6 @@
     to_sibling(1, 1, 2)
     arrive(0, 1, 2)
     to_sibling(0, 1, 2)
-    hidden(2)
 
     def backward(got, back, size, base, first_column):
         columns = RJ - first_column
@@ -377,8 +376,10 @@
     def gradients(chunk):
         chunk_cols = slice(chunk * RC, (chunk + 1) * RC)
         if chunk:
+            wait_cots(LATE, got_late, 1)
             backward(got_late, back_late, LATE, EARLY, RC)
         else:
+            wait_cots(EARLY, got_early, 0)
             backward(got_early, back_early, EARLY, 0, 0)
 
         @pl.loop(0, NE, unroll=8)
@@ -390,6 +391,9 @@
                 value = value + contract(back_late[rows, chunk_cols], hot_late[rows, :], 0, 0)
             weights[:, at(source * TOK, TOK)] = value.astype(BF)
 
+        if not chunk:
+            hidden(2)
+
         @pl.loop(0, D // 1024)
         def _(part):
             cols = at(part * 1024, 1024)
@@ -410,13 +414,10 @@
                     value = jnp.concatenate([grad_flat(base + quarter * QUARTER, size) for quarter in range(4)], axis=0)
                     col = 4 * offset + part * size
                     wire[chunk, share * 16:(share + 1) * 16, col:col + size] = value.astype(BF)
-            if chunk:
-                send_grads(1, wire_cols(sub), 1 + sub)
-        if not chunk:
-            send_grads(0, pl.ds(0, QUARTER), 0)
-
-    wait_cots(EARLY, got_early, 0)
+            send_grads(chunk, wire_cols(sub), 2 * chunk + sub)
+
     gradients(0)
+    gradients(1)
 
     exact = lax.Precision.HIGHEST
     start = 4 * UNITS * dp
@@ -459,9 +460,6 @@
     same = (line % 16 == lane // J) & (line // 16 != me)
     leave = ones(same & (line // 16 == dest // J))
     enter = ones(same & (line // 16 == owner // J))
-
-    wait_cots(LATE, got_late, 1)
-    gradients(1)
 
     loads[4].wait()
     loads[5].wait()
@@ -534,9 +532,9 @@
         ref = part_of(dy, dz, sub, half)
         copy_to(ref, ref, all_send.at[0], share_slot(dy, dz, sub, half), groups[0]).wait_recv()
 
-    wait_grads(0, pl.ds(0, QUARTER), 0)
     for sub in range(2):
-        wait_grads(1, wire_cols(sub), 1 + sub)
+        for chunk in range(2):
+            wait_grads(chunk, wire_cols(sub), 2 * chunk + sub)
         update(sub)
         move(0, pl.ds(*SUBS[sub]), sub)
     for sub in range(2):
@@ -571,7 +569,7 @@
         copy.wait_send()
 
 
-def finish_kernel(whole, first, second, new_a, new_b, new_first, new_second):
+def finish_kernel(whole, first, second, out_a, out_b, out_first, out_second, new_a, new_b, new_first, new_second, sems):
     index = iota((RJ, RJ), 0)
     turn = ones(iota((RJ, RJ), 1) == index % R * J + index // R)
 
@@ -589,15 +587,27 @@
             inside += size
         return parts[0] if len(parts) == 1 else jnp.concatenate(parts, axis=1)
 
-    for out, columns, base in ((new_a, A_UNITS, 0), (new_b, B_UNITS, A_UNITS * R)):
-        for column in range(columns):
-            stack = jnp.concatenate([unit(base + r * columns + column) for r in range(R)], axis=0).astype(BF)
-            out[:, column * UNIT:(column + 1) * UNIT] = jnp.dot(turn, stack, preferred_element_type=F32)
-    for out, value in ((new_first, first), (new_second, second)):
+    copies = []
+
+    def write(src, dst):
+        copy = pltpu.make_async_copy(src, dst, sems.at[len(copies)])
+        copy.start()
+        copies.append(copy)
+
+    for kept, out, value in ((new_first, out_first, first), (new_second, out_second, second)):
         for pair in range(8):
             both = value[pair * 16:(pair + 1) * 16, :].astype(F32)
-            out[:, 2 * pair * PIECE:(2 * pair + 1) * PIECE] = both[:J]
-            out[:, (2 * pair + 1) * PIECE:(2 * pair + 2) * PIECE] = both[J:]
+            kept[:, 2 * pair * PIECE:(2 * pair + 1) * PIECE] = both[:J]
+            kept[:, (2 * pair + 1) * PIECE:(2 * pair + 2) * PIECE] = both[J:]
+        write(kept, out)
+    for kept, out, columns, base in ((new_a, out_a, A_UNITS, 0), (new_b, out_b, B_UNITS, A_UNITS * R)):
+        for column in range(columns):
+            cols = pl.ds(column * UNIT, UNIT)
+            stack = jnp.concatenate([unit(base + r * columns + column) for r in range(R)], axis=0).astype(BF)
+            kept[:, cols] = jnp.dot(turn, stack, preferred_element_type=F32)
+            write(kept.at[:, cols], out.at[:, cols])
+    for copy in copies:
+        copy.wait()
 
 
 def vmem(count):
@@ -660,8 +670,8 @@
             dma((64,)),
             dma((32,)),
             dma((16,)),
-            dma((3 * ND,)),
-            dma((3 * ND,)),
+            dma((4 * ND,)),
+            dma((4 * ND,)),
             dma((4 * NE,)),
             dma((4 * NE,)),
             dma((32,)),
@@ -682,7 +692,14 @@
             jax.ShapeDtypeStruct((J, SHARE), F32),
         ],
         in_specs=vmem(3),
-        out_specs=vmem(4),
+        out_specs=anywhere(4),
+        scratch_shapes=[
+            pltpu.VMEM((RJ, D), F32),
+            pltpu.VMEM((RJ, FF), F32),
+            pltpu.VMEM((J, SHARE), F32),
+            pltpu.VMEM((J, SHARE), F32),
+            dma((2 + A_UNITS + B_UNITS,)),
+        ],
         compiler_params=pltpu.CompilerParams(vmem_limit_bytes=60 * 2**20),
         name="finish",
     )(whole, first, second)

time: 190 us -> 185 us (0.974)
  the two profiles are of different devices: /device:TPU:28 before, /device:TPU:1 now
where the time goes in v4:
time: 185 us; the launch traced here: 182 us
  Pallas kernels  181 us (98%)
    pallas_call x1, Pallas kernels, shards(): pl.pallas_call(main_kernel, out_shape=[jax.ShapeDtypeStruct((ND * 128, PI...  176 us
    pallas_call x1, Pallas kernels, shards(): pl.pallas_call(finish_kernel, out_shape=[jax.ShapeDtypeStruct((RJ, D), F3...  5.22 us

profile of v4, /device:TPU:1, one launch (start us, length us, event | category | flops | bytes accessed | tf_op | source)
XLA Modules:
  0.0 181.9 jit_solution(14957001026295973923)
XLA Ops:
  0.6 175.9 %dispatch_update.1 = (bf16[1024,1408]{1,0:T(8,128)(2,1)}, bf16[128,1408]{1,0:T(8,128)(2,1)}, bf16[128,1408]{1,0:T(8,128)(2,1)}) custom-call(bf16[128,4096]{1,0:T(8,128)(2,1)} %tok.1, bf16[1024,1536]{1,0:T(8,128)(2,1)} %bitcast.9, f32[8,128]{1,0:T(8,128)} %bitcast.11, s32[8,128]{1,0:T(8,128)} %bitcast.12, s32[1,128]{1,0:T(1,128)} %bitcast.13, ...), custom_call_target="tpu_custom_call" | custom-call | tf_op jit(solution)/shard_map/dispatch_update/pallas_call | solution.py:623
  176.5 5.2 %finish.1 = (f32[256,4096]{1,0:T(8,128)}, f32[256,1536]{1,0:T(8,128)}, f32[8,22528]{1,0:T(8,128)}, f32[8,22528]{1,0:T(8,128)}) custom-call(bf16[1024,1408]{1,0:T(8,128)(2,1)} %get-tuple-element.11.whole, bf16[128,1408]{1,0:T(8,128)(2,1)} %get-tuple-element.12.first, bf16[128,1408]{1,0:T(8,128)(2,1)} %get-tuple-element.13.second), custom_call_target="tpu_custom_call" | custom-call | tf_op jit(solution)/shard_map/finish/pallas_call | solution.py:686

commit v5 on v4

--- a/solution.py
+++ b/solution.py
@@ -24,16 +24,18 @@
 NE = 16
 ND = 8
 ROWS = J * CAP
-EARLY = 48
-LATE = ROWS - EARLY
+MSG = 16
+MESSAGES = ROWS // MSG
+BLOCK = NE * MSG
 RJ = R * J
-CH = 4
+CH = 2
+CHUNKS = J // CH
 RC = R * CH
 UNIT = 512
 SHARE = 22528
 PIECE = SHARE // 16
-QUARTER = SHARE // 4
-UNITS = QUARTER // UNIT
+EIGHTH = SHARE // 8
+UNITS = SHARE // UNIT
 A_UNITS = D // UNIT
 B_UNITS = FF // UNIT
 SPLIT = 1792
@@ -63,8 +65,8 @@
 
 def main_kernel(
     tok, up_hbm, gate_t, ids_t, homes_row, a_hbm, b_hbm, first_hbm, second_hbm, whole, first_out, second_out,
-    gathered, cots, send, got_early, got_late, ids_all, a, b, a16, b16, pick, hot_early, hot_late, low, weights,
-    low_early, low_late, back_early, back_late, grad_a, grad_b, row, wire, wire_got,
+    gathered, cots, send, got, ids_all, a, b, a16, b16, pick, hot, low, weights,
+    lows, back, grad_a, grad_b, row, wire, wire_got,
     first, second, rows_a, rows_b, param, moving, packed, landed,
     local, ids_send, ids_recv, cot_send, cot_recv, tok_send, tok_recv, sib_recv,
     grad_send, grad_recv, move_send, move_recv, all_send, all_recv,
@@ -204,22 +206,20 @@
 
     cot_sent = []
 
-    def send_cots(low_row, high_row, got, index):
-        size = high_row - low_row
-        for part in range(size // 16):
-            for peer in peers:
-                copy = copy_to(
-                    send.at[at(place(*peer) * ROWS + low_row + part * 16, 16)], got.at[at(me * size + part * 16, 16)],
-                    cot_send.at[len(cot_sent)], cot_recv.at[index * NE + me], device(*peer),
-                )
-                copy.start()
-                cot_sent.append(copy)
-        got[at(me * size, size, 16), :] = send[at(me * ROWS + low_row, size, 16), :]
-
-    def wait_cots(size, got, index):
+    def send_cots(message):
         for peer in peers:
-            ref = got.at[at(place(*peer) * size, size, 16)]
-            copy_to(ref, ref, cot_send.at[0], cot_recv.at[index * NE + place(*peer)], device(*peer)).wait_recv()
+            copy = copy_to(
+                send.at[at(place(*peer) * ROWS + message * MSG, MSG)], got.at[at(message * BLOCK + me * MSG, MSG)],
+                cot_send.at[len(cot_sent)], cot_recv.at[message * NE + me], device(*peer),
+            )
+            copy.start()
+            cot_sent.append(copy)
+        got[at(message * BLOCK + me * MSG, MSG), :] = send[at(me * ROWS + message * MSG, MSG), :]
+
+    def wait_cots(message):
+        for peer in peers:
+            ref = got.at[at(message * BLOCK + place(*peer) * MSG, MSG)]
+            copy_to(ref, ref, cot_send.at[0], cot_recv.at[message * NE + place(*peer)], device(*peer)).wait_recv()
 
     arrive(1, 1, 0)
     to_right(1, 1, 0)
@@ -233,7 +233,7 @@
     to_left(0, 0, 1, 1)
     to_across(0, 1)
     to_sibling(0, 0, 1)
-    send_cots(0, EARLY, got_early, 0)
+    send_cots(0)
 
     index = iota((RJ, RJ), 0)
     turn = ones(iota((RJ, RJ), 1) == (index // RC * CH + index % CH) * R + (index % RC) // CH)
@@ -259,10 +259,9 @@
     to_left(1, 0, 1, 1)
     to_sibling(1, 0, 1)
 
-    def own(size, base, columns, first_column):
-        line = iota((size, columns), 0) + base
-        column = iota((size, columns), 1) + first_column
-        return line // CAP == column // RC * CH + column % CH
+    def own(size, first_row, chunk):
+        line = iota((size, RC), 0) + first_row
+        return line // CAP == chunk * CH + iota((size, RC), 1) % CH
 
     def from_sibling(dx):
         for half in range(2):
@@ -275,12 +274,19 @@
         base = (x + dx) % 4
         rows = at(base * 4 * TOK, 4 * TOK)
         low[...] = contract(gathered[rows, :], a16[...], 1, 1).astype(BF)
-        for hots, lows, size, first_row in ((hot_early, low_early, EARLY, 0), (hot_late, low_late, LATE, EARLY)):
-            mask = own(size, first_row, RJ, 0)
-            for inside in range(4):
-                rows = at((base * 4 + inside) * size, size, 16)
-                value = jnp.dot(hots[rows, :], low[inside * TOK:(inside + 1) * TOK, :], preferred_element_type=F32)
-                lows[rows, :] = jnp.where(mask, value, 0.0).astype(BF)
+        for inside in range(4):
+            source = base * 4 + inside
+            value = jnp.dot(
+                hot[at(source * ROWS, ROWS, MSG), :], low[inside * TOK:(inside + 1) * TOK, :], preferred_element_type=F32
+            )
+            for chunk in range(CHUNKS):
+                first_row = chunk * MSG
+                part = jnp.where(
+                    own(2 * MSG, first_row, chunk),
+                    value[first_row:first_row + 2 * MSG, chunk * RC:(chunk + 1) * RC], 0.0,
+                ).astype(BF)
+                lows[chunk, at(source * MSG, MSG), :] = part[:MSG]
+                lows[chunk, at(BLOCK + source * MSG, MSG), :] = part[MSG:]
 
     arrive(0, 0, 2, 0)
     arrive(0, 0, 2, 1)
@@ -307,19 +313,60 @@
             hit = hit + jnp.where(ids[k:k + 1, :] == iota((J, TOK), 0) + me * J, 1.0, 0.0)
         count = jnp.dot(hit.astype(BF), before, preferred_element_type=F32)
         value = jnp.where(hit > 0.5, count, -1.0)
-        hot = ones(jnp.dot(repeat, value.astype(BF), preferred_element_type=F32) == turn_in)
-        hot_early[at(source * EARLY, EARLY), :] = hot[:EARLY]
-        hot_late[at(source * LATE, LATE), :] = hot[EARLY:]
+        found = ones(jnp.dot(repeat, value.astype(BF), preferred_element_type=F32) == turn_in)
+        hot[at(source * ROWS, ROWS, MSG), :] = found
+
+    exact = lax.Precision.HIGHEST
+    start = UNITS * dp
+    a_first = jnp.minimum(start // A_UNITS, R - 8)
+    b_first = jnp.clip((start - A_UNITS * R) // B_UNITS, 0, R - 16)
+
+    def chooser(count, base):
+        index = iota((count * J, RJ), 0)
+        return (iota((count * J, RJ), 1) == (index % J) * R + index // J + base).astype(F32)
+
+    @pl.loop(0, A_UNITS)
+    def _(part):
+        cols = at(part * UNIT, UNIT)
+        rows_a[:, cols] = jnp.dot(chooser(8, a_first), a[:, cols], preferred_element_type=F32, precision=exact)
+
+    @pl.loop(0, B_UNITS)
+    def _(part):
+        cols = at(part * UNIT, UNIT)
+        rows_b[:, cols] = jnp.dot(chooser(16, b_first), b[:, cols], preferred_element_type=F32, precision=exact)
+
+    @pl.loop(0, UNITS)
+    def _(column):
+        number = start + column
+        in_a = jnp.clip(number // A_UNITS - a_first, 0, 7)
+        number_b = jnp.maximum(number - A_UNITS * R, 0)
+        in_b = jnp.clip(number_b // B_UNITS - b_first, 0, 15)
+        value_a = rows_a[at(in_a * J, J), at(number % A_UNITS * UNIT, UNIT)]
+        value_b = rows_b[at(in_b * J, J), at(number_b % B_UNITS * UNIT, UNIT)]
+        param[:, at(column * UNIT, UNIT)] = jnp.where(number < A_UNITS * R, value_a, value_b)
+
+    homes_now = homes_row[...].astype(F32).astype(BF)
+    lane = iota((128, 128), 1)
+    line = iota((128, 128), 0)
+    dest = jnp.dot(homes_now, ones(line == me * J + lane % J), preferred_element_type=F32).astype(I32)
+    named = ones(homes_row[...] == me * J + line % J)
+    owner = contract(ones(iota((1, 128), 1) >= 0) * iota((1, 128), 1).astype(F32).astype(BF), named, 1, 1).astype(I32)
+    stay = ones((line // J == lane // J) & (line % J == owner % J) & (owner // J == me))
+    lane = iota((256, 128), 1)
+    line = iota((256, 128), 0)
+    same = (line % 16 == lane // J) & (line // 16 != me)
+    leave = ones(same & (line // 16 == dest // J))
+    enter = ones(same & (line // 16 == owner // J))
 
     hidden(0)
     arrive(0, 1, 3)
     to_sibling(0, 1, 3)
     arrive(0, 1, 1)
     to_sibling(0, 1, 1)
+    send_cots(1)
     arrive(1, 0, 2, 0)
     arrive(1, 0, 2, 1)
     to_sibling(1, 0, 2)
-    send_cots(EARLY, ROWS, got_late, 1)
     hidden(3)
     hidden(1)
     arrive(1, 1, 2, 0)
@@ -327,16 +374,8 @@
     to_sibling(1, 1, 2)
     arrive(0, 1, 2)
     to_sibling(0, 1, 2)
-
-    def backward(got, back, size, base, first_column):
-        columns = RJ - first_column
-        mask = jnp.concatenate([own(size, base, columns, first_column)] * 4, axis=0)
-
-        @pl.loop(0, 4)
-        def _(part):
-            rows = at(part * (4 * size), 4 * size)
-            value = contract(got[rows, :], b16[first_column:, :], 1, 1)
-            back[rows, first_column:] = jnp.where(mask, value, 0.0).astype(BF)
+    send_cots(2)
+    hidden(2)
 
     def grad_flat(number, size):
         parts = []
@@ -371,28 +410,28 @@
             copy_to(ref, ref, grad_send.at[0], grad_recv.at[index * ND + source], groups[step - 1]).wait_recv()
 
     def wire_cols(sub):
-        return pl.ds(4 * SUBS[sub][0], 4 * SUBS[sub][1])
+        return pl.ds(0, EIGHTH) if sub is None else pl.ds(2 * SUBS[sub][0], 2 * SUBS[sub][1])
 
     def gradients(chunk):
-        chunk_cols = slice(chunk * RC, (chunk + 1) * RC)
-        if chunk:
-            wait_cots(LATE, got_late, 1)
-            backward(got_late, back_late, LATE, EARLY, RC)
-        else:
-            wait_cots(EARLY, got_early, 0)
-            backward(got_early, back_early, EARLY, 0, 0)
+        used = pl.ds(chunk * BLOCK, 2 * BLOCK)
+        mask = [
+            jnp.concatenate([own(MSG, (chunk + message) * MSG, chunk)] * 4, axis=0) for message in range(2)
+        ]
+        for message in range(2):
+            for part in range(4):
+                rows = pl.ds((chunk + message) * BLOCK + part * 4 * MSG, 4 * MSG)
+                value = contract(got[rows, :], b16[chunk * RC:(chunk + 1) * RC, :], 1, 1)
+                value = jnp.where(mask[message], value, 0.0).astype(BF)
+                for inside in range(4):
+                    row0 = (part * 4 + inside) * 2 * MSG + message * MSG
+                    back[row0:row0 + MSG, :] = value[inside * MSG:(inside + 1) * MSG, :]
 
         @pl.loop(0, NE, unroll=8)
         def _(source):
-            rows = at(source * EARLY, EARLY)
-            value = contract(back_early[rows, chunk_cols], hot_early[rows, :], 0, 0)
-            if chunk:
-                rows = at(source * LATE, LATE)
-                value = value + contract(back_late[rows, chunk_cols], hot_late[rows, :], 0, 0)
+            value = contract(
+                back[at(source * 2 * MSG, 2 * MSG), :], hot[at(source * ROWS + chunk * MSG, 2 * MSG, MSG), :], 0, 0
+            )
             weights[:, at(source * TOK, TOK)] = value.astype(BF)
-
-        if not chunk:
-            hidden(2)
 
         @pl.loop(0, D // 1024)
         def _(part):
@@ -402,64 +441,32 @@
         @pl.loop(0, B_UNITS)
         def _(part):
             cols = at(part * UNIT, UNIT)
-            value = contract(low_early[:, chunk_cols], got_early[:, cols], 0, 0)
-            if chunk:
-                value = value + contract(low_late[:, chunk_cols], got_late[:, cols], 0, 0)
-            grad_b[:, cols] = value
-
+            grad_b[:, cols] = contract(lows[chunk], got[used, cols], 0, 0)
+
+        last = chunk == CHUNKS - 1
         for sub, (offset, size) in enumerate(SUBS):
             for share in range(ND):
-                for part in range(4):
+                for part in range(2):
                     base = share * SHARE + part * PIECE + offset
-                    value = jnp.concatenate([grad_flat(base + quarter * QUARTER, size) for quarter in range(4)], axis=0)
-                    col = 4 * offset + part * size
+                    value = jnp.concatenate([grad_flat(base + eighth * EIGHTH, size) for eighth in range(8)], axis=0)
+                    col = 2 * offset + part * size
                     wire[chunk, share * 16:(share + 1) * 16, col:col + size] = value.astype(BF)
-            send_grads(chunk, wire_cols(sub), 2 * chunk + sub)
-
+            if last:
+                send_grads(chunk, wire_cols(sub), chunk + sub)
+        if not last:
+            send_grads(chunk, wire_cols(None), chunk)
+
+    wait_cots(0)
+    send_cots(3)
+    wait_cots(1)
     gradients(0)
+    wait_cots(2)
+    send_cots(4)
     gradients(1)
-
-    exact = lax.Precision.HIGHEST
-    start = 4 * UNITS * dp
-    a_first = jnp.minimum(start // A_UNITS, R - 8)
-    b_first = jnp.clip((start - A_UNITS * R) // B_UNITS, 0, R - 16)
-
-    def chooser(count, base):
-        index = iota((count * J, RJ), 0)
-        return (iota((count * J, RJ), 1) == (index % J) * R + index // J + base).astype(F32)
-
-    @pl.loop(0, A_UNITS)
-    def _(part):
-        cols = at(part * UNIT, UNIT)
-        rows_a[:, cols] = jnp.dot(chooser(8, a_first), a[:, cols], preferred_element_type=F32, precision=exact)
-
-    @pl.loop(0, B_UNITS)
-    def _(part):
-        cols = at(part * UNIT, UNIT)
-        rows_b[:, cols] = jnp.dot(chooser(16, b_first), b[:, cols], preferred_element_type=F32, precision=exact)
-
-    @pl.loop(0, 4 * UNITS)
-    def _(column):
-        number = start + column
-        in_a = jnp.clip(number // A_UNITS - a_first, 0, 7)
-        number_b = jnp.maximum(number - A_UNITS * R, 0)
-        in_b = jnp.clip(number_b // B_UNITS - b_first, 0, 15)
-        value_a = rows_a[at(in_a * J, J), at(number % A_UNITS * UNIT, UNIT)]
-        value_b = rows_b[at(in_b * J, J), at(number_b % B_UNITS * UNIT, UNIT)]
-        param[:, at(column * UNIT, UNIT)] = jnp.where(number < A_UNITS * R, value_a, value_b)
-
-    homes_now = homes_row[...].astype(F32).astype(BF)
-    lane = iota((128, 128), 1)
-    line = iota((128, 128), 0)
-    dest = jnp.dot(homes_now, ones(line == me * J + lane % J), preferred_element_type=F32).astype(I32)
-    named = ones(homes_row[...] == me * J + line % J)
-    owner = contract(ones(iota((1, 128), 1) >= 0) * iota((1, 128), 1).astype(F32).astype(BF), named, 1, 1).astype(I32)
-    stay = ones((line // J == lane // J) & (line % J == owner % J) & (owner // J == me))
-    lane = iota((256, 128), 1)
-    line = iota((256, 128), 0)
-    same = (line % 16 == lane // J) & (line // 16 != me)
-    leave = ones(same & (line // 16 == dest // J))
-    enter = ones(same & (line // 16 == owner // J))
+    wait_cots(3)
+    gradients(2)
+    wait_cots(4)
+    gradients(3)
 
     loads[4].wait()
     loads[5].wait()
@@ -468,18 +475,18 @@
 
     def update(sub):
         offset, size = SUBS[sub]
-        for part in range(4):
-            inside = pl.ds(4 * offset + part * size, size)
+        for part in range(2):
+            inside = pl.ds(2 * offset + part * size, size)
             totals = []
-            for chunk in range(2):
+            for chunk in range(CHUNKS):
                 grad = wire_got[chunk, 0:16, inside].astype(F32)
                 for source in range(1, ND):
                     grad = grad + wire_got[chunk, source * 16:(source + 1) * 16, inside].astype(F32)
                 totals.append(adapter_scale_factor * grad)
-            for quarter in range(4):
-                piece = quarter * 4 + part
+            for eighth in range(8):
+                piece = eighth * 2 + part
                 cols = pl.ds(piece * PIECE + offset, size)
-                grad = jnp.concatenate([total[quarter * CH:(quarter + 1) * CH] for total in totals], axis=0)
+                grad = jnp.concatenate([total[eighth * CH:(eighth + 1) * CH] for total in totals], axis=0)
                 one = beta_one * first[:, cols] + (1.0 - beta_one) * grad
                 two = beta_two * second[:, cols] + (1.0 - beta_two) * grad * grad
                 old = param[:, cols]
@@ -532,9 +539,10 @@
         ref = part_of(dy, dz, sub, half)
         copy_to(ref, ref, all_send.at[0], share_slot(dy, dz, sub, half), groups[0]).wait_recv()
 
+    for chunk in range(CHUNKS - 1):
+        wait_grads(chunk, wire_cols(None), chunk)
     for sub in range(2):
-        for chunk in range(2):
-            wait_grads(chunk, wire_cols(sub), 2 * chunk + sub)
+        wait_grads(CHUNKS - 1, wire_cols(sub), CHUNKS - 1 + sub)
         update(sub)
         move(0, pl.ds(*SUBS[sub]), sub)
     for sub in range(2):
@@ -633,27 +641,23 @@
             pltpu.VMEM((NE * TOK, D), BF),
             pltpu.VMEM((COPIES, FF), BF),
             pltpu.VMEM((NE * ROWS, FF), BF),
-            pltpu.VMEM((NE * EARLY, FF), BF),
-            pltpu.VMEM((NE * LATE, FF), BF),
+            pltpu.VMEM((NE * ROWS, FF), BF),
             pltpu.VMEM((NE * TOP, TOK), I32),
             pltpu.VMEM((RJ, D), F32),
             pltpu.VMEM((RJ, FF), F32),
             pltpu.VMEM((RJ, D), BF),
             pltpu.VMEM((RJ, FF), BF),
             pltpu.VMEM((4 * ROWS, COPIES), BF),
-            pltpu.VMEM((NE * EARLY, TOK), BF),
-            pltpu.VMEM((NE * LATE, TOK), BF),
+            pltpu.VMEM((NE * ROWS, TOK), BF),
             pltpu.VMEM((4 * TOK, RJ), BF),
             pltpu.VMEM((RC, NE * TOK), BF),
-            pltpu.VMEM((NE * EARLY, RJ), BF),
-            pltpu.VMEM((NE * LATE, RJ), BF),
-            pltpu.VMEM((NE * EARLY, RJ), BF),
-            pltpu.VMEM((NE * LATE, RJ), BF),
+            pltpu.VMEM((CHUNKS, 2 * BLOCK, RC), BF),
+            pltpu.VMEM((2 * BLOCK, RC), BF),
             pltpu.VMEM((RC, D), F32),
             pltpu.VMEM((RC, FF), F32),
             pltpu.VMEM((1, COPIES), I32),
-            pltpu.VMEM((2, ND * 16, QUARTER), BF),
-            pltpu.VMEM((2, ND * 16, QUARTER), BF),
+            pltpu.VMEM((CHUNKS, ND * 16, EIGHTH), BF),
+            pltpu.VMEM((CHUNKS, ND * 16, EIGHTH), BF),
             pltpu.VMEM((J, SHARE), F32),
             pltpu.VMEM((J, SHARE), F32),
             pltpu.VMEM((8 * J, D), F32),
@@ -666,12 +670,12 @@
             dma((NE,)),
             dma((NE,)),
             dma((NE * 5,)),
-            dma((2 * NE,)),
+            dma((MESSAGES * NE,)),
             dma((64,)),
             dma((32,)),
             dma((16,)),
-            dma((4 * ND,)),
-            dma((4 * ND,)),
+            dma(((CHUNKS + 1) * ND,)),
+            dma(((CHUNKS + 1) * ND,)),
             dma((4 * NE,)),
             dma((4 * NE,)),
             dma((32,)),

time: 185 us -> 179 us (0.968); the launches traced: 182 us -> 178 us
  Pallas kernels: 181 us -> 178 us
    pallas_call x1, Pallas kernels: 176 us -> 172 us  [shards(): pl.pallas_call(main_kernel, out_shape=[jax.ShapeDtypeStruct((ND * 128, PI...]
where the time goes in v5:
time: 179 us; the launch traced here: 178 us
  Pallas kernels  178 us (99%)
    pallas_call x1, Pallas kernels, shards(): pl.pallas_call(main_kernel, out_shape=[jax.ShapeDtypeStruct((ND * 128, PI...  172 us
    pallas_call x1, Pallas kernels, shards(): pl.pallas_call(finish_kernel, out_shape=[jax.ShapeDtypeStruct((RJ, D), F3...  5.23 us

profile of v5, /device:TPU:1, one launch (start us, length us, event | category | flops | bytes accessed | tf_op | source)
XLA Modules:
  0.0 178.4 jit_solution(851052147649170672)
XLA Ops:
  0.6 172.4 %dispatch_update.1 = (bf16[1024,1408]{1,0:T(8,128)(2,1)}, bf16[128,1408]{1,0:T(8,128)(2,1)}, bf16[128,1408]{1,0:T(8,128)(2,1)}) custom-call(bf16[128,4096]{1,0:T(8,128)(2,1)} %tok.1, bf16[1024,1536]{1,0:T(8,128)(2,1)} %bitcast.9, f32[8,128]{1,0:T(8,128)} %bitcast.11, s32[8,128]{1,0:T(8,128)} %bitcast.12, s32[1,128]{1,0:T(1,128)} %bitcast.13, ...), custom_call_target="tpu_custom_call" | custom-call | tf_op jit(solution)/shard_map/dispatch_update/pallas_call | solution.py:631
  173.1 5.2 %finish.1 = (f32[256,4096]{1,0:T(8,128)}, f32[256,1536]{1,0:T(8,128)}, f32[8,22528]{1,0:T(8,128)}, f32[8,22528]{1,0:T(8,128)}) custom-call(bf16[1024,1408]{1,0:T(8,128)(2,1)} %get-tuple-element.11.whole, bf16[128,1408]{1,0:T(8,128)(2,1)} %get-tuple-element.12.first, bf16[128,1408]{1,0:T(8,128)(2,1)} %get-tuple-element.13.second), custom_call_target="tpu_custom_call" | custom-call | tf_op jit(solution)/shard_map/finish/pallas_call | solution.py:690

commit v6 on v5

--- a/solution.py
+++ b/solution.py
@@ -39,7 +39,7 @@
 A_UNITS = D // UNIT
 B_UNITS = FF // UNIT
 SPLIT = 1792
-SUBS = ((0, 768), (768, 640))
+SUBS = ((0, 640), (640, 768))
 
 MESH = pl.DeviceIdType.MESH
 BF = jnp.bfloat16
@@ -65,7 +65,7 @@
 
 def main_kernel(
     tok, up_hbm, gate_t, ids_t, homes_row, a_hbm, b_hbm, first_hbm, second_hbm, whole, first_out, second_out,
-    gathered, cots, send, got, ids_all, a, b, a16, b16, pick, hot, low, weights,
+    gathered, cots, send, got, ids_all, a, b, a16, b16, pick, hot, low, weights, picked,
     lows, back, grad_a, grad_b, row, wire, wire_got,
     first, second, rows_a, rows_b, param, moving, packed, landed,
     local, ids_send, ids_recv, cot_send, cot_recv, tok_send, tok_recv, sib_recv,
@@ -418,6 +418,8 @@
             jnp.concatenate([own(MSG, (chunk + message) * MSG, chunk)] * 4, axis=0) for message in range(2)
         ]
         for message in range(2):
+            if message:
+                wait_cots(chunk + 1)
             for part in range(4):
                 rows = pl.ds((chunk + message) * BLOCK + part * 4 * MSG, 4 * MSG)
                 value = contract(got[rows, :], b16[chunk * RC:(chunk + 1) * RC, :], 1, 1)
@@ -426,24 +428,30 @@
                     row0 = (part * 4 + inside) * 2 * MSG + message * MSG
                     back[row0:row0 + MSG, :] = value[inside * MSG:(inside + 1) * MSG, :]
 
-        @pl.loop(0, NE, unroll=8)
-        def _(source):
-            value = contract(
-                back[at(source * 2 * MSG, 2 * MSG), :], hot[at(source * ROWS + chunk * MSG, 2 * MSG, MSG), :], 0, 0
-            )
-            weights[:, at(source * TOK, TOK)] = value.astype(BF)
-
-        @pl.loop(0, D // 1024)
-        def _(part):
-            cols = at(part * 1024, 1024)
-            grad_a[:, cols] = jnp.dot(weights[...], gathered[:, cols], preferred_element_type=F32)
+        last = chunk == CHUNKS - 1
+        if last:
+            @pl.loop(0, D // 1024)
+            def _(part):
+                cols = at(part * 1024, 1024)
+                grad_a[:, cols] = contract(back[...], picked[:, cols], 0, 0)
+        else:
+            @pl.loop(0, NE, unroll=8)
+            def _(source):
+                value = contract(
+                    back[at(source * 2 * MSG, 2 * MSG), :], hot[at(source * ROWS + chunk * MSG, 2 * MSG, MSG), :], 0, 0
+                )
+                weights[:, at(source * TOK, TOK)] = value.astype(BF)
+
+            @pl.loop(0, D // 1024)
+            def _(part):
+                cols = at(part * 1024, 1024)
+                grad_a[:, cols] = jnp.dot(weights[...], gathered[:, cols], preferred_element_type=F32)
 
         @pl.loop(0, B_UNITS)
         def _(part):
             cols = at(part * UNIT, UNIT)
             grad_b[:, cols] = contract(lows[chunk], got[used, cols], 0, 0)
 
-        last = chunk == CHUNKS - 1
         for sub, (offset, size) in enumerate(SUBS):
             for share in range(ND):
                 for part in range(2):
@@ -458,14 +466,20 @@
 
     wait_cots(0)
     send_cots(3)
-    wait_cots(1)
+
+    @pl.loop(0, NE)
+    def _(source):
+        rows = at(source * TOK, TOK)
+        mark = hot[at(source * ROWS + (CHUNKS - 1) * MSG, 2 * MSG, MSG), :]
+        for part in range(D // 1024):
+            cols = pl.ds(part * 1024, 1024)
+            picked[at(source * 2 * MSG, 2 * MSG), cols] = jnp.dot(mark, gathered[rows, cols], preferred_element_type=F32).astype(BF)
+
+
     gradients(0)
-    wait_cots(2)
     send_cots(4)
     gradients(1)
-    wait_cots(3)
     gradients(2)
-    wait_cots(4)
     gradients(3)
 
     loads[4].wait()
@@ -496,9 +510,11 @@
 
     move_sent = []
 
-    def move(kind, cols, index):
+    def pack_moves(kind, cols):
         packed[kind, :, cols] = jnp.dot(leave, moving[kind, :, cols], preferred_element_type=F32).astype(BF)
         landed[kind, at(me * 16, 16), cols] = jnp.zeros((16, cols.size), BF)
+
+    def move(kind, cols, index):
         for step in (8, 9, 10, 11, 7, 6, 5, 4, 12, 13, 14, 15, 3, 2, 1):
             to = homes[step - 1]
             copy = copy_to(
@@ -544,29 +560,40 @@
     for sub in range(2):
         wait_grads(CHUNKS - 1, wire_cols(sub), CHUNKS - 1 + sub)
         update(sub)
+        pack_moves(0, pl.ds(*SUBS[sub]))
         move(0, pl.ds(*SUBS[sub]), sub)
-    for sub in range(2):
+    full = pl.ds(0, PIECE)
+    pack_moves(1, full)
+    pack_moves(2, full)
+
+    def begin(sub):
         cols = pl.ds(*SUBS[sub])
         whole[at(dp * 128, 128), cols] = arrived(0, cols, sub)
         pass_on(0, 0, sub, 1, 0)
         pass_on(0, 0, sub, 0, 1)
         pass_on(0, 0, sub, 0, 3)
-    full = pl.ds(0, PIECE)
-    move(1, full, 2)
-    move(2, full, 3)
-    for sub in range(2):
+
+    def across(sub):
         came(1, 0, sub)
         pass_on(1, 0, sub, 0, 1)
         pass_on(1, 0, sub, 0, 3)
-        came(0, 3, sub)
-        pass_on(0, 3, sub, 0, 1, 0)
-        came(0, 1, sub)
-        pass_on(0, 1, sub, 0, 3, 1)
-    for sub in range(2):
-        came(1, 3, sub)
-        pass_on(1, 3, sub, 0, 1, 0)
-        came(1, 1, sub)
-        pass_on(1, 1, sub, 0, 3, 1)
+
+    def around(dy, sub):
+        came(dy, 3, sub)
+        pass_on(dy, 3, sub, 0, 1, 0)
+        came(dy, 1, sub)
+        pass_on(dy, 1, sub, 0, 3, 1)
+
+    begin(0)
+    across(0)
+    begin(1)
+    around(0, 0)
+    move(1, full, 2)
+    across(1)
+    around(1, 0)
+    move(2, full, 3)
+    around(0, 1)
+    around(1, 1)
     first_out[...] = arrived(1, full, 2)
     second_out[...] = arrived(2, full, 3)
     for sub in range(2):
@@ -651,6 +678,7 @@
             pltpu.VMEM((NE * ROWS, TOK), BF),
             pltpu.VMEM((4 * TOK, RJ), BF),
             pltpu.VMEM((RC, NE * TOK), BF),
+            pltpu.VMEM((2 * BLOCK, D), BF),
             pltpu.VMEM((CHUNKS, 2 * BLOCK, RC), BF),
             pltpu.VMEM((2 * BLOCK, RC), BF),
             pltpu.VMEM((RC, D), F32),

time: 179 us -> 175 us (0.978)
  Pallas kernels: 178 us -> 174 us
    pallas_call x1, Pallas kernels: 172 us -> 169 us  [shards(): pl.pallas_call(main_kernel, out_shape=[jax.ShapeDtypeStruct((ND * 128, PI...]
where the time goes in v6:
time: 175 us
  Pallas kernels  174 us (99%)
    pallas_call x1, Pallas kernels, shards(): pl.pallas_call(main_kernel, out_shape=[jax.ShapeDtypeStruct((ND * 128, PI...  169 us
    pallas_call x1, Pallas kernels, shards(): pl.pallas_call(finish_kernel, out_shape=[jax.ShapeDtypeStruct((RJ, D), F3...  5.22 us

profile of v6, /device:TPU:1, one launch (start us, length us, event | category | flops | bytes accessed | tf_op | source)
XLA Modules:
  0.0 174.6 jit_solution(87004025933358864)
XLA Ops:
  0.6 168.5 %dispatch_update.1 = (bf16[1024,1408]{1,0:T(8,128)(2,1)}, bf16[128,1408]{1,0:T(8,128)(2,1)}, bf16[128,1408]{1,0:T(8,128)(2,1)}) custom-call(bf16[128,4096]{1,0:T(8,128)(2,1)} %tok.1, bf16[1024,1536]{1,0:T(8,128)(2,1)} %bitcast.9, f32[8,128]{1,0:T(8,128)} %bitcast.11, s32[8,128]{1,0:T(8,128)} %bitcast.12, s32[1,128]{1,0:T(1,128)} %bitcast.13, ...), custom_call_target="tpu_custom_call" | custom-call | tf_op jit(solution)/shard_map/dispatch_update/pallas_call | solution.py:658
  169.2 5.2 %finish.1 = (f32[256,4096]{1,0:T(8,128)}, f32[256,1536]{1,0:T(8,128)}, f32[8,22528]{1,0:T(8,128)}, f32[8,22528]{1,0:T(8,128)}) custom-call(bf16[1024,1408]{1,0:T(8,128)(2,1)} %get-tuple-element.11.whole, bf16[128,1408]{1,0:T(8,128)(2,1)} %get-tuple-element.12.first, bf16[128,1408]{1,0:T(8,128)(2,1)} %get-tuple-element.13.second), custom_call_target="tpu_custom_call" | custom-call | tf_op jit(solution)/shard_map/finish/pallas_call | solution.py:718

commit v7 on v6

--- a/solution.py
+++ b/solution.py
@@ -39,7 +39,7 @@
 A_UNITS = D // UNIT
 B_UNITS = FF // UNIT
 SPLIT = 1792
-SUBS = ((0, 640), (640, 768))
+SUBS = ((0, 768), (768, 640))
 
 MESH = pl.DeviceIdType.MESH
 BF = jnp.bfloat16
@@ -588,11 +588,11 @@
     across(0)
     begin(1)
     around(0, 0)
+    across(1)
     move(1, full, 2)
-    across(1)
     around(1, 0)
+    around(0, 1)
     move(2, full, 3)
-    around(0, 1)
     around(1, 1)
     first_out[...] = arrived(1, full, 2)
     second_out[...] = arrived(2, full, 3)

time: 175 us -> 178 us (1.017); the launches traced: 175 us -> 175 us
  no operation moved by 1% of the time
where the time goes in v7:
time: 178 us; the launch traced here: 175 us
  Pallas kernels  174 us (98%)
    pallas_call x1, Pallas kernels, shards(): pl.pallas_call(main_kernel, out_shape=[jax.ShapeDtypeStruct((ND * 128, PI...  169 us
    pallas_call x1, Pallas kernels, shards(): pl.pallas_call(finish_kernel, out_shape=[jax.ShapeDtypeStruct((RJ, D), F3...  5.22 us

profile of v7, /device:TPU:1, one launch (start us, length us, event | category | flops | bytes accessed | tf_op | source)
XLA Modules:
  0.0 175.2 jit_solution(12982335420715890245)
XLA Ops:
  0.6 169.2 %dispatch_update.1 = (bf16[1024,1408]{1,0:T(8,128)(2,1)}, bf16[128,1408]{1,0:T(8,128)(2,1)}, bf16[128,1408]{1,0:T(8,128)(2,1)}) custom-call(bf16[128,4096]{1,0:T(8,128)(2,1)} %tok.1, bf16[1024,1536]{1,0:T(8,128)(2,1)} %bitcast.9, f32[8,128]{1,0:T(8,128)} %bitcast.11, s32[8,128]{1,0:T(8,128)} %bitcast.12, s32[1,128]{1,0:T(1,128)} %bitcast.13, ...), custom_call_target="tpu_custom_call" | custom-call | tf_op jit(solution)/shard_map/dispatch_update/pallas_call | solution.py:658
  169.8 5.2 %finish.1 = (f32[256,4096]{1,0:T(8,128)}, f32[256,1536]{1,0:T(8,128)}, f32[8,22528]{1,0:T(8,128)}, f32[8,22528]{1,0:T(8,128)}) custom-call(bf16[1024,1408]{1,0:T(8,128)(2,1)} %get-tuple-element.11.whole, bf16[128,1408]{1,0:T(8,128)(2,1)} %get-tuple-element.12.first, bf16[128,1408]{1,0:T(8,128)(2,1)} %get-tuple-element.13.second), custom_call_target="tpu_custom_call" | custom-call | tf_op jit(solution)/shard_map/finish/pallas_call | solution.py:718
